TPU v7x, 32 devices: a whole 2x2x4 slice. The times are simulated.
32 devices in a mesh: groups: 2 (over x), tensor: 8 (over z, y), dp: 2 (over core).
Axes of the slice: x: 2, y: 2, z: 4, core: 2. Of those that a mesh axis runs over, the one named last changes fastest.
Arguments:
- cotangent: bfloat16 [2048, 8192], P(('groups', 'dp'), 'tensor'), parts along dimension 0, may hold values from -6 to 6
- activations: bfloat16 [2048, 32768], P(('groups', 'dp'), 'tensor'), parts along dimension 0, may hold values from -0.59765625 to 0.59765625
- qweight: int32 [32768, 4096], P('tensor'), may hold values from 0 to 255, as said below
- scales: bfloat16 [512, 8192], P('tensor'), may hold values from 0.0010986328 to 0.0047912598
- adapter_down_weight: bfloat16 [16, 16, 32768], P(('groups', 'tensor')), parts along dimension 0, may hold values from -0.23925781 to 0.23925781
- adapter_up_weight: bfloat16 [16, 16, 8192], P(('groups', 'tensor')), parts along dimension 0, may hold values from -0.0625 to 0.0625
- token_job_index: int32 [2048, 1], P(('groups', 'dp')), parts along dimension 0, may hold values from 0 to 7; in each aligned block of 512 rows (0 to 511, 512 to 1023, ...) at most 256 rows name the same one
- job_slot_owner: int32 [16], P('groups'), parts along dimension 0, may hold values from 0 to 7, each once
Outputs:
- grad_input: bfloat16 [2048, 32768], P(('groups', 'dp'), 'tensor'), parts along dimension 0
- grad_a: float32 [16, 16, 32768], P(('groups', 'tensor'), None, 'dp'), parts along dimension 0
- grad_b: float32 [16, 16, 8192], P(('groups', 'tensor'), None, 'dp'), parts along dimension 0
There are 2 independent parts, one for each index of `groups`. A program takes and returns all parts, laid end to end along the dimension named above; an argument that names none is the same for every part. Nothing has to cross between parts.
Inputs may be any that keep to these rules, and one draw needn't show every extreme that they name: `token_job_index`: among the 512 rows of one index of dp (aligned blocks of rows), no job is named by more than 256 rows; some job is named by exactly 256 rows. `job_slot_owner`: each slot is named once. `qweight`: every word holds two independent codes in its low eight bits.
All inputs are finite; a program needn't handle non-finite values.
Results may differ from a plain program's by a relative error of at most 0.0048.
Values may be sent and summed in bfloat16 or wider, within the bound.
No kernel may reach another device: no remote copies, remote signals or barrier semaphores. Data moves between devices by JAX's collectives and lax.ppermute only.
A program may use at most 960 MiB of HBM per device.

v0:
```python
import functools

import jax
import jax.numpy as jnp
from jax import lax
from jax.experimental import pallas as pl
from jax.experimental.pallas import tpu as pltpu
from jax.sharding import PartitionSpec as P

GROUP = 64
CHUNKS = 8
MIB = 2**20
bf16, f32 = jnp.bfloat16, jnp.float32
ANY = pl.BlockSpec(memory_space=pl.ANY)
VM = pl.BlockSpec(memory_space=pltpu.VMEM)


def params(mib):
    return pltpu.CompilerParams(vmem_limit_bytes=mib * MIB)


def cost(flops, nbytes):
    return pl.CostEstimate(flops=int(flops), bytes_accessed=int(nbytes), transcendentals=0)


def xdot(a, b, ca, cb):
    return lax.dot_general(a, b, (((ca,), (cb,)), ((), ())), preferred_element_type=f32)


def base_kernel(nc, first, last, low, wide, rows, whole_in, whole_out, ids, *refs):
    refs = list(refs)
    c_refs, q_refs, s_refs = refs[:nc], refs[nc : 2 * nc], refs[2 * nc : 3 * nc]
    refs = refs[3 * nc :]
    acc_ref = None if first else refs.pop(0)
    r_ref, d_ref = (refs.pop(0), refs.pop(0)) if low else (None, None)
    rin_ref = refs.pop(0) if wide else None
    cd, sd = refs[-2:]
    up_ref = refs[-3] if wide else None
    out_ref, token_ref = refs[-5:-3] if wide else refs[-4:-2]
    width = cd.shape[2]
    step = pl.program_id(0)

    @pl.when(step == 0)
    def _():
        row = lax.broadcasted_iota(jnp.int32, (256, 256), 0)
        col = lax.broadcasted_iota(jnp.int32, (256, 256), 1)
        perm = (row == 2 * (col % 128) + col // 128).astype(f32).astype(bf16)
        token_ref[...] = jnp.zeros_like(token_ref)
        for c in range(nc):
            if wide:
                at = pl.ds(pl.multiple_of(ids[c] * width, width), width)
                up_ref[:, at] = 2.0 * xdot(rin_ref[...], c_refs[c][...], 1, 0)
            for b in range(width // 256):
                at = slice(b * 256, b * 256 + 256)
                cd[c, :, at] = xdot(c_refs[c][:, at], perm, 1, 0).astype(bf16)
                sd[c, :, at] = xdot(s_refs[c][:, at], perm, 1, 0)

    total = None
    for c in range(nc):
        words = q_refs[c][...]
        srows = sd[c, pl.ds(pl.multiple_of(step * (rows // GROUP), rows // GROUP), rows // GROUP), :]
        parts = []
        for b in range(width // 256):
            word = words[:, b * 128 : b * 128 + 128]
            for half in range(2):
                code = (word & 15) if half == 0 else lax.shift_right_logical(word, 4)
                at = b * 256 + half * 128
                scale = jnp.broadcast_to(
                    srows[:, at : at + 128].astype(bf16)[:, None, :], (rows // GROUP, GROUP, 128)
                ).reshape(rows, 128)
                parts.append((code - 8).astype(bf16) * scale)
        weight = jnp.concatenate(parts, axis=1)
        term = xdot(cd[c], weight, 1, 1)
        total = term if total is None else total + term
    cols = pl.ds(pl.multiple_of(step * rows, rows), rows)
    if acc_ref is not None:
        total = total + (acc_ref[:, cols] if whole_in else acc_ref[...])
    if low:
        total = total + (2.0 * xdot(r_ref[...], d_ref[...], 1, 0)).astype(bf16).astype(f32)
    if whole_out:
        out_ref[:, cols] = total
    else:
        out_ref[...] = total.astype(out_ref.dtype)


def base_step(ids, chunks, q, s, acc=None, adapter=None, up=None, last=False, after=(), rows=1024, whole=(True, True), limit=24):
    nc = len(chunks)
    tok, width = chunks[0].shape
    hidden = q.shape[0]
    rows = min(rows, hidden)
    first = acc is None
    low, wide = adapter is not None, up is not None
    groups = s.shape[0]
    vm = pl.BlockSpec(memory_space=pltpu.VMEM)
    in_specs = [vm for _ in chunks]
    in_specs += [pl.BlockSpec((rows, width // 2), lambda i, ids, c=c: (i, ids[c])) for c in range(nc)]
    in_specs += [pl.BlockSpec((groups, width), lambda i, ids, c=c: (0, ids[c])) for c in range(nc)]
    args = list(chunks) + [q] * nc + [s] * nc
    aliases = {}
    whole_in, whole_out = whole[0], whole[1] and not last
    block = pl.BlockSpec((tok, rows), lambda i, ids: (0, i))
    if not first:
        if whole_in == whole_out and not last:
            aliases = {1 + len(args): 0}
        in_specs.append(vm if whole_in else block)
        args.append(acc)
    if low:
        ranks = adapter[0].shape[1]
        in_specs.append(pl.BlockSpec((tok, ranks), lambda i, ids: (0, 0)))
        in_specs.append(pl.BlockSpec((ranks, rows), lambda i, ids: (0, i)))
        args += list(adapter)
    out_specs = [
        vm if whole_out else block,
        pl.BlockSpec((8, 128), lambda i, ids: (0, 0)),
    ]
    out_shape = [
        jax.ShapeDtypeStruct((tok, hidden), bf16 if last else f32),
        jax.ShapeDtypeStruct((8, 128), f32),
    ]
    if wide:
        in_specs += [pl.BlockSpec(memory_space=pltpu.VMEM)] * 2
        aliases[2 + len(args)] = 2
        args += list(up)
        out_specs.append(vm)
        out_shape.append(jax.ShapeDtypeStruct(up[1].shape, f32))
    in_specs += [pl.BlockSpec(memory_space=pl.ANY)] * len(after)
    args += list(after)
    return pl.pallas_call(
        functools.partial(base_kernel, nc, first, last, low, wide, rows, whole_in, whole_out),
        grid_spec=pltpu.PrefetchScalarGridSpec(
            num_scalar_prefetch=1,
            grid=(hidden // rows,),
            in_specs=in_specs,
            out_specs=out_specs,
            scratch_shapes=[pltpu.VMEM((nc, tok, width), bf16), pltpu.VMEM((nc, groups, width), f32)],
        ),
        out_shape=out_shape,
        input_output_aliases=aliases,
        compiler_params=params(limit),
        cost_estimate=cost(1000, 1000),
    )(ids, *args)


def slots_of(job_ref, owner_ref, jobs):
    tok = job_ref[...]
    slot = jnp.zeros_like(tok)
    for k in range(jobs):
        slot = jnp.where(tok == k, owner_ref[k], slot)
    return slot


def pack_kernel(n, down_ref, up_ref, out_ref):
    core = lax.axis_index("dp")
    dcols, ucols = down_ref.shape[1] // (2 * n), up_ref.shape[1] // (2 * n)
    for r in range(n):
        at = pl.multiple_of((2 * r + core) * dcols, dcols)
        out_ref[r, :, :dcols] = down_ref[:, pl.ds(at, dcols)]
        at = pl.multiple_of((2 * r + core) * ucols, ucols)
        out_ref[r, :, dcols:] = up_ref[:, pl.ds(at, ucols)]


def pack(down, up, n):
    rank = down.shape[0]
    cols = (down.shape[1] + up.shape[1]) // (2 * n)
    return pl.pallas_call(
        functools.partial(pack_kernel, n),
        out_shape=jax.ShapeDtypeStruct((n, rank, cols), bf16),
        compiler_params=params(16),
        cost_estimate=cost(1000, 1000),
    )(down, up)


def ranks_kernel(n, rank, owner_ref, job_ref, act_ref, cot_ref, own_ref, got_ref, after, *refs):
    keep_ref, send_ref, d_ref, u_ref = refs
    me, core = lax.axis_index("tensor"), lax.axis_index("dp")
    slot = slots_of(job_ref, owner_ref, n)
    dcols, ucols = d_ref.shape[1] // 2, u_ref.shape[1] // 2
    for ref, which in ((own_ref, core), (got_ref, 1 - core)):
        d_ref[:, pl.ds(pl.multiple_of(which * dcols, dcols), dcols)] = ref[:, :, :dcols].reshape(-1, dcols)
        u_ref[:, pl.ds(pl.multiple_of(which * ucols, ucols), ucols)] = ref[:, :, dcols:].reshape(-1, ucols)
    rin = xdot(d_ref[...], act_ref[...], 1, 1)
    rout = xdot(u_ref[...], cot_ref[...], 1, 1)
    mine = jnp.zeros((rank, rout.shape[1]), f32)
    for r in range(n):
        mine = jnp.where(slot == r, rout[r * rank : (r + 1) * rank], mine)
    even = lax.rem(me, 2) == 0
    for z in range(n // 2):
        first = rin[2 * z * rank : (2 * z + 1) * rank]
        second = rin[(2 * z + 1) * rank : (2 * z + 2) * rank]
        keep_ref[z] = jnp.where(even, first, second)
        send_ref[z] = jnp.where(even, second, first)
    keep_ref[n // 2] = mine
    send_ref[n // 2] = mine


def ranks(owner, job, act, cot, own, got, after):
    n, rank, _ = own.shape
    tok, hidden = act.shape
    part = jax.ShapeDtypeStruct((n // 2 + 1, rank, tok), f32)
    return pl.pallas_call(
        functools.partial(ranks_kernel, n, rank),
        in_specs=[pl.BlockSpec(memory_space=pltpu.SMEM)] + [VM] * 5 + [ANY],
        out_specs=[VM] * 3,
        out_shape=[part, part, jax.ShapeDtypeStruct((n * rank, hidden), bf16)],
        scratch_shapes=[pltpu.VMEM((n * rank, cot.shape[1]), bf16)],
        compiler_params=params(16),
        cost_estimate=cost(1000, 1000),
    )(owner, job, act, cot, own, got, after)


def mix_kernel(n, keep_ref, got_ref, after, *outs):
    place = lax.axis_index("tensor") // 2
    rank = keep_ref.shape[1]
    rout = keep_ref[n // 2] + got_ref[n // 2]
    for r in range(n // 2):
        z = lax.bitwise_xor(place, r)
        outs[r][:rank] = keep_ref[z] + got_ref[z]
        outs[r][rank:] = rout


def mix(n, keep, got, after):
    _, rank, tok = keep.shape
    return pl.pallas_call(
        functools.partial(mix_kernel, n),
        in_specs=[VM, VM, ANY],
        out_specs=[VM] * (n // 2),
        out_shape=[jax.ShapeDtypeStruct((2 * rank, tok), f32)] * (n // 2),
        compiler_params=params(16),
        cost_estimate=cost(1000, 1000),
    )(keep, got, after)


def grads_kernel(n, rank, owner_ref, job_ref, act_ref, *refs):
    parts, (rin_ref, r_ref, keep_ref, send_ref) = refs[: n // 2], refs[-4:]
    me, core = lax.axis_index("tensor"), lax.axis_index("dp")
    slot = slots_of(job_ref, owner_ref, n)
    total = parts[0][...]
    for p in parts[1:]:
        total = total + p[...]
    rin_ref[...] = jnp.where(slot == me, total[:rank], 0.0).astype(bf16)
    rout = total[rank:].astype(bf16).astype(f32)
    spread = jnp.concatenate([jnp.where(slot == r, rout, 0.0) for r in range(n)], axis=0)
    r_ref[...] = spread.T.astype(bf16)
    left = spread.astype(bf16)
    half = act_ref.shape[1] // 2
    for ref, which in ((send_ref, 1 - core), (keep_ref, core)):
        cols = pl.ds(pl.multiple_of(which * half, half), half)
        ref[...] = (2.0 * xdot(left, act_ref[:, cols], 1, 0)).reshape(ref.shape)


def grads(owner, job, act, parts, after):
    n, rank = 2 * len(parts), parts[0].shape[0] // 2
    tok, hidden = act.shape
    half = jax.ShapeDtypeStruct((n, rank, hidden // 2), f32)
    return pl.pallas_call(
        functools.partial(grads_kernel, n, rank),
        in_specs=[pl.BlockSpec(memory_space=pltpu.SMEM)] + [VM] * (2 + n // 2) + [ANY],
        out_specs=[VM] * 4,
        out_shape=[
            jax.ShapeDtypeStruct((rank, tok), bf16),
            jax.ShapeDtypeStruct((tok, n * rank), bf16),
            half,
            half,
        ],
        compiler_params=params(16),
        cost_estimate=cost(1000, 1000),
    )(owner, job, act, *parts, after)


def split_kernel(keep_ref, got_ref, after, own_ref, send_ref):
    side = lax.rem(lax.axis_index("tensor"), 2)
    for z in range(own_ref.shape[0]):
        for ref, which in ((own_ref, side), (send_ref, 1 - side)):
            ref[z] = (keep_ref[2 * z + which] + got_ref[2 * z + which]).astype(bf16)


def split(keep, got, after):
    n, rank, cols = keep.shape
    return pl.pallas_call(
        split_kernel,
        in_specs=[VM, VM, ANY],
        out_specs=[VM, VM],
        out_shape=[jax.ShapeDtypeStruct((n // 2, rank, cols), bf16)] * 2,
        compiler_params=params(16),
        cost_estimate=cost(1000, 1000),
    )(keep, got, after)


def merge_kernel(own_ref, got_ref, after, *outs):
    z, core = lax.axis_index("tensor") // 2, lax.axis_index("dp")
    for r, out in enumerate(outs):
        to = lax.bitwise_xor(lax.rem(z, 2) * 2 + core, r)
        out[0] = own_ref[to]
        out[1] = got_ref[to]


def merge(own, got, after):
    rounds, rank, cols = own.shape
    return pl.pallas_call(
        merge_kernel,
        in_specs=[VM, VM, ANY],
        out_specs=[VM] * rounds,
        out_shape=[jax.ShapeDtypeStruct((2, rank, cols), bf16)] * rounds,
        compiler_params=params(16),
        cost_estimate=cost(1000, 1000),
    )(own, got, after)


def join_kernel(*refs):
    parts, out_ref = refs[:-2], refs[-1]
    me = lax.axis_index("tensor")
    cols = parts[0].shape[2]
    for r, part in enumerate(parts):
        source = lax.bitwise_xor(me // 2, r)
        for other in range(2):
            side = lax.bitwise_xor(lax.rem(me, 2), other)
            block = (source // 2) * 2 + side
            at = pl.multiple_of((block * 2 + lax.rem(source, 2)) * cols, cols)
            out_ref[0, :, pl.ds(at, cols)] = part[other].astype(f32)


def join(parts, after):
    _, rank, cols = parts[0].shape
    return pl.pallas_call(
        join_kernel,
        in_specs=[VM] * len(parts) + [ANY],
        out_shape=jax.ShapeDtypeStruct((1, rank, 2 * len(parts) * cols), f32),
        compiler_params=params(16),
        cost_estimate=cost(1000, 1000),
    )(*parts, after)


def tie_kernel(*refs):
    pass


def tie(arrays, after, spec):
    n = len(arrays)
    return pl.pallas_call(
        tie_kernel,
        in_specs=[spec] * n + [ANY],
        out_specs=[spec] * n,
        out_shape=[jax.ShapeDtypeStruct(x.shape, x.dtype) for x in arrays],
        input_output_aliases={i: i for i in range(n)},
        compiler_params=params(16),
        cost_estimate=cost(1000, 1000),
    )(*arrays, after)


def cut_kernel(right_ref, left_ref, after, top_ref, bottom_ref):
    half = top_ref.shape[0]
    top_ref[...] = right_ref[:half]
    bottom_ref[...] = left_ref[half:]


def cut(right, left, after):
    half = jax.ShapeDtypeStruct((right.shape[0] // 2, right.shape[1]), right.dtype)
    return pl.pallas_call(
        cut_kernel,
        in_specs=[VM, VM, ANY],
        out_specs=[VM, VM],
        out_shape=[half, half],
        compiler_params=params(16),
        cost_estimate=cost(1000, 1000),
    )(right, left, after)


def up_kernel(nc, ids, rin_ref, *refs):
    chunks, out_ref = refs[:nc], refs[-1]
    width = chunks[0].shape[1]
    for c in range(nc):
        at = pl.ds(pl.multiple_of(ids[c] * width, width), width)
        out_ref[:, at] = 2.0 * xdot(rin_ref[...], chunks[c][...], 1, 0)


def up_step(ids, rin, chunks, after):
    nc = len(chunks)
    width = chunks[0].shape[1]
    vm = pl.BlockSpec(memory_space=pltpu.VMEM)
    return pl.pallas_call(
        functools.partial(up_kernel, nc),
        in_specs=[pl.BlockSpec(memory_space=pltpu.SMEM)] + [vm] * (nc + 1) + [ANY],
        out_specs=vm,
        out_shape=jax.ShapeDtypeStruct((rin.shape[0], CHUNKS * width), f32),
        compiler_params=params(16),
        cost_estimate=cost(1000, 1000),
    )(ids, rin, *chunks, after)


def up_last_kernel(ids, rin_ref, chunk_ref, up_ref, after, keep_ref, send_ref):
    core = lax.axis_index("dp")
    width = chunk_ref.shape[1]
    half = keep_ref.shape[1]
    each = half // width
    term = 2.0 * xdot(rin_ref[...], chunk_ref[...], 1, 0)
    at = pl.ds(pl.multiple_of(lax.rem(ids[0], each) * width, width), width)
    for ref, which in ((keep_ref, core), (send_ref, 1 - core)):
        ref[...] = up_ref[:, pl.ds(pl.multiple_of(which * half, half), half)]

        @pl.when(ids[0] // each == which)
        def _():
            ref[:, at] = term


def up_last(ids, rin, chunk, up, after):
    vm = pl.BlockSpec(memory_space=pltpu.VMEM)
    half = jax.ShapeDtypeStruct((up.shape[0], up.shape[1] // 2), f32)
    return pl.pallas_call(
        up_last_kernel,
        in_specs=[pl.BlockSpec(memory_space=pltpu.SMEM)] + [vm] * 3 + [ANY],
        out_specs=[vm, vm],
        out_shape=[half, half],
        compiler_params=params(16),
        cost_estimate=cost(1000, 1000),
    )(ids, rin, chunk, up, after)


def small_ring(cot, act, q, scales, down, up, job, owner, n):
    rank = down.shape[0]
    ring = list(range(0, n, 2)) + list(range(n - 1, 0, -2))
    forth = [(ring[i], ring[(i + 1) % n]) for i in range(n)]
    back = [(b, a) for a, b in forth]
    table = []
    for j in range(n):
        p = ring.index(j)
        order = [j]
        for h in range(1, n // 2):
            order += [ring[(p - h) % n], ring[(p + h) % n]]
        table.append(order + [ring[(p + n // 2) % n]])
    me = lax.axis_index("tensor")
    ids = lax.dynamic_index_in_dim(jnp.array(table, jnp.int32), me, 0, keepdims=False)
    swap = [(0, 1), (1, 0)]

    def ring_step(right, left):
        return lax.ppermute(right, "tensor", forth), lax.ppermute(left, "tensor", back)

    def exchange(x):
        return lax.all_to_all(x, "tensor", split_axis=0, concat_axis=0, tiled=True)

    job_row = job.reshape(1, -1)
    def xor(x, r):
        return lax.ppermute(x, "tensor", [(j, j ^ r) for j in range(n)])

    pairs = [ids[2 * h - 1 : 2 * h + 1] for h in range(1, n // 2)]

    right1, left1 = ring_step(cot, cot)
    pieces = exchange(pack(down, up, n))
    other = lax.ppermute(pieces, "dp", swap)
    acc, token = base_step(ids[:1], [cot], q, scales, after=[pieces])
    keep, send, down_cols = ranks(owner, job_row, act, cot, pieces, other, token)
    got = xor(send, 1)

    right1, left1 = tie((right1, left1), down_cols, VM)
    right2, left2 = ring_step(right1, left1)
    acc, token = base_step(pairs[0], [right1, left1], q, scales, acc, after=[down_cols])
    mixed = mix(n, keep, got, token)
    parts = [mixed[0]] + [xor(mixed[r], 2 * r) for r in range(1, n // 2)]

    right2, left2 = tie((right2, left2), mixed[0], VM)
    right3, left3 = ring_step(right2, left2)
    acc, token = base_step(pairs[1], [right2, left2], q, scales, acc, after=[mixed[0]])
    rin, spread, keep, send = grads(owner, job_row, act, parts, token)
    got = lax.ppermute(send, "dp", swap)

    halves = ring_step(*cut(right3, left3, rin))
    grad_up = up_step(ids[:5], rin, [cot, right1, left1, right2, left2], rin)
    own, send = split(keep, got, grad_up)
    got = xor(send, 1)
    acc, token, grad_up = base_step(
        pairs[2], [right3, left3], q, scales, acc, (spread, down_cols), (rin, grad_up), after=[own]
    )
    routed = []
    for r, piece in enumerate(merge(own, got, token)):
        hops = []
        for z in range(n // 2):
            for y in range(2):
                for core in range(2):
                    to = ((z % 2) * 2 + core) ^ r
                    hops.append((z * 4 + y * 2 + core, to * 4 + y * 2 + z // 2))
        routed.append(lax.ppermute(piece, ("tensor", "dp"), hops))
    last = jnp.concatenate(tie(halves, token, VM), axis=0)
    keep, send = up_last(ids[n - 1 :], rin, last, grad_up, token)
    other = lax.ppermute(send, "dp", swap)
    grad_input, token = base_step(ids[n - 1 :], [last], q, scales, acc, last=True, after=[keep])
    grad_a = join(routed, token)
    return grad_input, grad_a, (keep + other)[None]


def large_ring(cot, act, q, scales, down, up, job, owner, n):
    rank = down.shape[0]
    me = lax.axis_index("tensor")
    jobs = owner.shape[0]
    hit = (job == jnp.arange(jobs, dtype=jnp.int32)[None, :]).astype(jnp.int32)
    slot = jnp.sum(hit * owner[None, :], axis=1)
    full = lax.all_gather(cot, "tensor", axis=1, tiled=True)
    down_cols = lax.all_to_all(
        down.reshape(rank, n, -1), "tensor", split_axis=1, concat_axis=0, tiled=True
    ).reshape(n * rank, -1)
    up_cols = lax.all_to_all(
        up.reshape(rank, n, -1), "tensor", split_axis=1, concat_axis=0, tiled=True
    ).reshape(n * rank, -1)
    mask = jnp.repeat(slot[:, None] == jnp.arange(n, dtype=jnp.int32)[None, :], rank, axis=1)
    rin = lax.psum_scatter(xdot(down_cols, act, 1, 1), "tensor", scatter_dimension=0, tiled=True)
    rin = jnp.where((slot == me)[None, :], rin, 0.0).astype(bf16)
    rout = lax.psum(jnp.where(mask, xdot(cot, up_cols, 1, 1), 0.0), "tensor")
    spread = rout.astype(bf16)
    grad_a = 2.0 * xdot(spread, act, 0, 0)
    grad_a = lax.all_to_all(grad_a, "tensor", split_axis=0, concat_axis=1, tiled=True)
    grad_a = lax.psum_scatter(grad_a, "dp", scatter_dimension=1, tiled=True)[None]
    grad_b = 2.0 * xdot(rin, full, 1, 0)
    grad_b = lax.psum_scatter(grad_b, "dp", scatter_dimension=1, tiled=True)[None]
    width = full.shape[1] // CHUNKS
    ids = jnp.arange(CHUNKS, dtype=jnp.int32)
    chunks = [full[:, c * width : (c + 1) * width] for c in range(CHUNKS)]
    acc, _ = base_step(ids[:2], chunks[:2], q, scales)
    for c in range(2, CHUNKS - 2, 2):
        acc, _ = base_step(ids[c : c + 2], chunks[c : c + 2], q, scales, acc)
    grad_input, _ = base_step(
        ids[CHUNKS - 2 :], chunks[CHUNKS - 2 :], q, scales, acc, (spread, down_cols), last=True
    )
    return grad_input, grad_a, grad_b


def solution(mesh):
    n = mesh.shape["tensor"]

    def on_device(cot, act, q, scales, down, up, job, owner):
        path = small_ring if n == CHUNKS == 8 and mesh.shape["dp"] == 2 else large_ring
        return path(cot, act, q, scales, down[0], up[0], job, owner, n)

    return jax.shard_map(
        on_device,
        mesh=mesh,
        in_specs=(
            P(("groups", "dp"), "tensor"),
            P(("groups", "dp"), "tensor"),
            P("tensor", None),
            P("tensor", None),
            P(("groups", "tensor"), None, None),
            P(("groups", "tensor"), None, None),
            P(("groups", "dp"), None),
            P("groups"),
        ),
        out_specs=(
            P(("groups", "dp"), "tensor"),
            P(("groups", "tensor"), None, "dp"),
            P(("groups", "tensor"), None, "dp"),
        ),
        check_vma=False,
    )
```

profile of v0, /device:TPU:0, one launch (start us, length us, event | category | flops | bytes accessed | tf_op | source)
XLA Modules:
  0.0 151.0 jit_solution(10215648937959533211)
XLA Ops:
  0.6 1.2 copy-done.4
  1.9 0.9 copy-done.5
  2.8 0.9 shard_map.112
  3.7 7.3 %all-to-all-start = ((bf16[8,16,2560]{2,1,0:T(8,128)(2,1)}), bf16[8,16,2560]{2,1,0:T(8,128)(2,1)S(1)}, u32[]{:S(2)}, u32[]{:S(2)}) async-start(bf16[8,16,2560]{2,1,0:T(8,128)(2,1)} %shard_map.112), calls=%async_computation | async-start | bytes 1310720 | tf_op jit(solution)/shard_map/all_to_all | solution.py:438
  11.0 2.0 %collective-permute-start = (bf16[512,1024]{1,0:T(8,128)(2,1)}, bf16[512,1024]{1,0:T(8,128)(2,1)S(1)}, u32[]{:S(2)}, u32[]{:S(2)}) collective-permute-start(bf16[512,1024]{1,0:T(8,128)(2,1)} %refs_0_.3), channel_id=1, source_target_pairs={{0,4},{4,8},{8,12},{12,14},{14,10},{10,6},{6,2},{2,0},{1,5},{5,9},... | collective-permute-start | bytes 3145736 | tf_op jit(solution)/shard_map/ppermute | solution.py:435
  13.0 16.7 %all-to-all-done.refs_3_.own_ref = bf16[8,16,2560]{2,1,0:T(8,128)(2,1)S(1)} async-done(((bf16[8,16,2560]{2,1,0:T(8,128)(2,1)}), bf16[8,16,2560]{2,1,0:T(8,128)(2,1)S(1)}, u32[]{:S(2)}, u32[]{:S(2)}) %all-to-all-start) | async-done | bytes 655392 | tf_op jit(solution)/shard_map/all_to_all | solution.py:438
  29.7 0.7 constant_dynamic-slice_fusion
  31.0 1.2 copy-done
  32.2 1.2 copy-done.2
  33.5 9.0 %shard_map.113 = (f32[512,4096]{1,0:T(8,128)S(1)}, f32[8,128]{1,0:T(8,128)S(1)}) custom-call(s32[1]{0:T(128)} %bitcast.4.ids, bf16[512,1024]{1,0:T(8,128)(2,1)S(1)} %copy-done.2, s32[4096,4096]{1,0:T(8,128)} %refs_1_.3, bf16[64,8192]{1,0:T(8,128)(2,1)S(1)} %copy-done, bf16[8,16,2560]{2,1,0:T(8,128)(2,1)S(1)} %all-to-all-done.refs_3_.own_ref), custom_call_target="tpu_custom_call" | custom-call | flops 1000 | bytes 1000 | tf_op jit(solution)/shard_map/pallas_call | solution.py:128
  42.5 2.4 %shard_map.114 = (f32[5,16,512]{2,1,0:T(8,128)S(1)}, f32[5,16,512]{2,1,0:T(8,128)S(1)}, bf16[128,4096]{1,0:T(8,128)(2,1)S(1)}) custom-call(s32[8]{0:T(128)S(1)} %copy-done.7, s32[1,512]{1,0:T(1,128)S(1)} %bitcast.17, bf16[512,4096]{1,0:T(8,128)(2,1)S(1)} %copy-done.1, bf16[512,1024]{1,0:T(8,128)(2,1)S(1)} %copy-done.3, ...), custom_call_target="tpu_custom_call" | custom-call | flops 1000 | bytes 1000 | tf_op jit(solution)/shard_map/pallas_call | solution.py:200
  45.0 1.3 collective-permute-done.1.refs_1_
  46.3 5.0 %collective-permute-start.3 = (bf16[512,1024]{1,0:T(8,128)(2,1)S(1)}, bf16[512,1024]{1,0:T(8,128)(2,1)S(1)}, u32[]{:S(2)}, u32[]{:S(2)}) collective-permute-start(bf16[512,1024]{1,0:T(8,128)(2,1)S(1)} %get-tuple-element.43.refs_0_.refs_1_), channel_id=1, source_target_pairs={{0,4},{4,8},{8,12},{12,14},{14,10},{10,6},{6,2},{2,0},{1,5},{5,9},... | collective-permute-start | bytes 3145736 | tf_op jit(solution)/shard_map/ppermute | solution.py:435
  51.3 1.5 %collective-permute-start.5 = (f32[5,16,512]{2,1,0:T(8,128)S(1)}, f32[5,16,512]{2,1,0:T(8,128)S(1)}, u32[]{:S(2)}, u32[]{:S(2)}) collective-permute-start(f32[5,16,512]{2,1,0:T(8,128)S(1)} %get-tuple-element.46), channel_id=1, source_target_pairs={{0,2},{2,0},{4,6},{6,4},{8,10},{10,8},{12,14},{14,12},{1,3},{3,1},... | collective-permute-start | bytes 491528 | tf_op jit(solution)/shard_map/ppermute | solution.py:442
  52.9 14.1 %shard_map.116 = (f32[512,4096]{1,0:T(8,128)S(1)}, f32[8,128]{1,0:T(8,128)S(1)}) custom-call(s32[2]{0:T(128)S(1)} %get-tuple-element.81.ids, bf16[512,1024]{1,0:T(8,128)(2,1)S(1)} %get-tuple-element.43.refs_0_.refs_1_, bf16[512,1024]{1,0:T(8,128)(2,1)S(1)} %get-tuple-element.44.refs_1_.refs_2_, ...), custom_call_target="tpu_custom_call", output_to_operand_aliasing={{0}: (7, {})} | custom-call | flops 1000 | bytes 1000 | tf_op jit(solution)/shard_map/pallas_call | solution.py:128
  67.0 9.1 %collective-permute-done.5.got_ref = f32[5,16,512]{2,1,0:T(8,128)S(1)} collective-permute-done((f32[5,16,512]{2,1,0:T(8,128)S(1)}, f32[5,16,512]{2,1,0:T(8,128)S(1)}, u32[]{:S(2)}, u32[]{:S(2)}) %collective-permute-start.5) | collective-permute-done | bytes 163872 | tf_op jit(solution)/shard_map/ppermute | solution.py:442
  76.2 2.5 %collective-permute-start.7 = (bf16[512,1024]{1,0:T(8,128)(2,1)S(1)}, bf16[512,1024]{1,0:T(8,128)(2,1)S(1)}, u32[]{:S(2)}, u32[]{:S(2)}) collective-permute-start(bf16[512,1024]{1,0:T(8,128)(2,1)S(1)} %get-tuple-element.51.refs_1_.refs_4_), channel_id=1, source_target_pairs={{4,0},{8,4},{12,8},{14,12},{10,14},{6,10},{2,6},{0,2},{5,1},{9,5},... | collective-permute-start | bytes 3145736 | tf_op jit(solution)/shard_map/ppermute | solution.py:435
  78.7 4.3 %collective-permute-start.10 = (f32[32,512]{1,0:T(8,128)S(1)}, f32[32,512]{1,0:T(8,128)S(1)}, u32[]{:S(2)}, u32[]{:S(2)}) collective-permute-start(f32[32,512]{1,0:T(8,128)S(1)} %get-tuple-element.54), channel_id=1, source_target_pairs={{0,12},{2,14},{4,8},{6,10},{8,4},{10,6},{12,0},{14,2},{1,13},{3,15... | collective-permute-start | bytes 196616 | tf_op jit(solution)/shard_map/ppermute | solution.py:442
  83.6 14.1 %shard_map.119 = (f32[512,4096]{1,0:T(8,128)S(1)}, f32[8,128]{1,0:T(8,128)S(1)}) custom-call(s32[2]{0:T(128)S(1)} %get-tuple-element.80.ids, bf16[512,1024]{1,0:T(8,128)(2,1)S(1)} %get-tuple-element.50.refs_0_.refs_3_, bf16[512,1024]{1,0:T(8,128)(2,1)S(1)} %get-tuple-element.51.refs_1_.refs_4_, ...), custom_call_target="tpu_custom_call", output_to_operand_aliasing={{0}: (7, {})} | custom-call | flops 1000 | bytes 1000 | tf_op jit(solution)/shard_map/pallas_call | solution.py:128
  97.7 10.2 %collective-permute-done.10.refs_3_ = f32[32,512]{1,0:T(8,128)S(1)} collective-permute-done((f32[32,512]{1,0:T(8,128)S(1)}, f32[32,512]{1,0:T(8,128)S(1)}, u32[]{:S(2)}, u32[]{:S(2)}) %collective-permute-start.10) | collective-permute-done | bytes 65568 | tf_op jit(solution)/shard_map/ppermute | solution.py:442
  107.8 1.5 %collective-permute-done.9.refs_2_ = f32[32,512]{1,0:T(8,128)S(1)} collective-permute-done((f32[32,512]{1,0:T(8,128)S(1)}, f32[32,512]{1,0:T(8,128)S(1)}, u32[]{:S(2)}, u32[]{:S(2)}) %collective-permute-start.9) | collective-permute-done | bytes 65568 | tf_op jit(solution)/shard_map/ppermute | solution.py:442
  109.4 1.3 shard_map.120
  111.3 1.6 %collective-permute-start.12 = (bf16[256,1024]{1,0:T(8,128)(2,1)S(1)}, bf16[256,1024]{1,0:T(8,128)(2,1)S(1)}, u32[]{:S(2)}, u32[]{:S(2)}) collective-permute-start(bf16[256,1024]{1,0:T(8,128)(2,1)S(1)} %get-tuple-element.59), channel_id=1, source_target_pairs={{4,0},{8,4},{12,8},{14,12},{10,14},{6,10},{2,6},{0,2},{5,1},{9,5},... | collective-permute-start | bytes 1572872 | tf_op jit(solution)/shard_map/ppermute | solution.py:435
  112.9 1.3 shard_map.122.after.refs_10_
  114.4 15.7 %shard_map.124 = (f32[512,4096]{1,0:T(8,128)S(1)}, f32[8,128]{1,0:T(8,128)S(1)}, f32[16,8192]{1,0:T(8,128)S(1)}) custom-call(s32[2]{0:T(128)S(1)} %get-tuple-element.79.ids, bf16[512,1024]{1,0:T(8,128)(2,1)S(1)} %collective-permute-done.6.right_ref.refs_0_, ...), custom_call_target="tpu_custom_call", output_to_operand_aliasing={{0}: (7, {}), {2}: (11, {})} | custom-call | flops 1000 | bytes 1000 | tf_op jit(solution)/shard_map/pallas_call | solution.py:128
  130.3 0.9 shard_map.126
  132.0 2.1 %collective-permute-start.16 = (bf16[2,16,2048]{2,1,0:T(8,128)(2,1)S(1)}, bf16[2,16,2048]{2,1,0:T(8,128)(2,1)S(1)}, u32[]{:S(2)}, u32[]{:S(2)}) collective-permute-start(bf16[2,16,2048]{2,1,0:T(8,128)(2,1)S(1)} %get-tuple-element.74), channel_id=1, source_target_pairs={{0,4},{1,0},{2,6},{3,2},{4,12},{5,8},{6,14},{7,10},{8,5},{9,1},{10... | collective-permute-start | bytes 393224 | tf_op jit(solution)/shard_map/ppermute | solution.py:480
  134.1 2.2 %collective-permute-start.17 = (bf16[2,16,2048]{2,1,0:T(8,128)(2,1)S(1)}, bf16[2,16,2048]{2,1,0:T(8,128)(2,1)S(1)}, u32[]{:S(2)}, u32[]{:S(2)}) collective-permute-start(bf16[2,16,2048]{2,1,0:T(8,128)(2,1)S(1)} %get-tuple-element.75), channel_id=1, source_target_pairs={{0,8},{1,12},{2,10},{3,14},{4,0},{5,4},{6,2},{7,6},{8,9},{9,13},{1... | collective-permute-start | bytes 393224 | tf_op jit(solution)/shard_map/ppermute | solution.py:480
  136.4 2.9 %collective-permute-start.18 = (bf16[2,16,2048]{2,1,0:T(8,128)(2,1)S(1)}, bf16[2,16,2048]{2,1,0:T(8,128)(2,1)S(1)}, u32[]{:S(2)}, u32[]{:S(2)}) collective-permute-start(bf16[2,16,2048]{2,1,0:T(8,128)(2,1)S(1)} %get-tuple-element.76), channel_id=1, source_target_pairs={{0,12},{1,8},{2,14},{3,10},{4,4},{5,0},{6,6},{7,2},{8,13},{9,9},{1... | collective-permute-start | bytes 393224 | tf_op jit(solution)/shard_map/ppermute | solution.py:480
  139.3 9.9 %shard_map.127 = (bf16[512,4096]{1,0:T(8,128)(2,1)}, f32[8,128]{1,0:T(8,128)S(1)}) custom-call(s32[1]{0:T(128)} %bitcast.ids, bf16[512,1024]{1,0:T(8,128)(2,1)S(1)} %constant_dynamic-update-slice_fusion.chunk_ref.refs_0_, s32[4096,4096]{1,0:T(8,128)} %refs_1_.3, bf16[64,8192]{1,0:T(8,128)(2,1)S(1)} %copy-done, f32[512,4096]{1,0:T(8,128)S(1)} %get-tuple-element.68.refs_3_, ...), custom_call_target="tpu_custom_call" | custom-call | flops 1000 | bytes 1000 | tf_op jit(solution)/shard_map/pallas_call | solution.py:128
  149.2 1.1 shard_map.129
  150.3 0.7 add_bitcast_fusion
  (51 shorter events, 3.1 us)
Async XLA Ops:
  0.6 1.2 copy-start.4
  1.9 0.9 copy-start.5
  3.7 26.0 %all-to-all-start = ((bf16[8,16,2560]{2,1,0:T(8,128)(2,1)}), bf16[8,16,2560]{2,1,0:T(8,128)(2,1)S(1)}, u32[]{:S(2)}, u32[]{:S(2)}) async-start(bf16[8,16,2560]{2,1,0:T(8,128)(2,1)} %shard_map.112), calls=%async_computation | async-start | bytes 1310720 | tf_op jit(solution)/shard_map/all_to_all | solution.py:438
  11.0 34.0 %collective-permute-start = (bf16[512,1024]{1,0:T(8,128)(2,1)}, bf16[512,1024]{1,0:T(8,128)(2,1)S(1)}, u32[]{:S(2)}, u32[]{:S(2)}) collective-permute-start(bf16[512,1024]{1,0:T(8,128)(2,1)} %refs_0_.3), channel_id=1, source_target_pairs={{0,4},{4,8},{8,12},{12,14},{14,10},{10,6},{6,2},{2,0},{1,5},{5,9},... | collective-permute-start | bytes 3145736 | tf_op jit(solution)/shard_map/ppermute | solution.py:435
  13.0 33.3 %collective-permute-start.1 = (bf16[512,1024]{1,0:T(8,128)(2,1)}, bf16[512,1024]{1,0:T(8,128)(2,1)S(1)}, u32[]{:S(2)}, u32[]{:S(2)}) collective-permute-start(bf16[512,1024]{1,0:T(8,128)(2,1)} %refs_0_.3), channel_id=1, source_target_pairs={{4,0},{8,4},{12,8},{14,12},{10,14},{6,10},{2,6},{0,2},{5,1},{9,5},... | collective-permute-start | bytes 3145736 | tf_op jit(solution)/shard_map/ppermute | solution.py:435
  29.7 12.7 %collective-permute-start.2 = (bf16[8,16,2560]{2,1,0:T(8,128)(2,1)S(1)}, bf16[8,16,2560]{2,1,0:T(8,128)(2,1)S(1)}, u32[]{:S(2)}, u32[]{:S(2)}) collective-permute-start(bf16[8,16,2560]{2,1,0:T(8,128)(2,1)S(1)} %all-to-all-done.refs_3_.own_ref), channel_id=1, source_target_pairs={{0,1},{1,0},{2,3},{3,2},{4,5},{5,4},{6,7},{7,6},{8,9},{9,8},{10,11... | collective-permute-start | bytes 1966088 | tf_op jit(solution)/shard_map/ppermute | solution.py:448
  31.0 1.2 copy-start
  32.2 1.2 copy-start.2
  33.5 9.0 %copy-start.1 = (bf16[512,4096]{1,0:T(8,128)(2,1)S(1)}, bf16[512,4096]{1,0:T(8,128)(2,1)}, u32[]{:S(2)}) copy-start(bf16[512,4096]{1,0:T(8,128)(2,1)} %act_ref.3) | copy-start | bytes 12582916
  33.5 9.0 %copy-start.3 = (bf16[512,1024]{1,0:T(8,128)(2,1)S(1)}, bf16[512,1024]{1,0:T(8,128)(2,1)}, u32[]{:S(2)}) copy-start(bf16[512,1024]{1,0:T(8,128)(2,1)} %refs_0_.3) | copy-start | bytes 3145732
  33.5 9.0 %copy-start.6 = (s32[512,1]{0,1:T(1,128)S(1)}, s32[512,1]{0,1:T(1,128)}, u32[]{:S(2)}) copy-start(s32[512,1]{0,1:T(1,128)} %param.15) | copy-start | bytes 6148
  33.5 9.1 %copy-start.7 = (s32[8]{0:T(128)S(1)}, s32[8]{0:T(128)}, u32[]{:S(2)}) copy-start(s32[8]{0:T(128)} %owner_ref.3) | copy-start | bytes 100
  46.3 29.8 %collective-permute-start.3 = (bf16[512,1024]{1,0:T(8,128)(2,1)S(1)}, bf16[512,1024]{1,0:T(8,128)(2,1)S(1)}, u32[]{:S(2)}, u32[]{:S(2)}) collective-permute-start(bf16[512,1024]{1,0:T(8,128)(2,1)S(1)} %get-tuple-element.43.refs_0_.refs_1_), channel_id=1, source_target_pairs={{0,4},{4,8},{8,12},{12,14},{14,10},{10,6},{6,2},{2,0},{1,5},{5,9},... | collective-permute-start | bytes 3145736 | tf_op jit(solution)/shard_map/ppermute | solution.py:435
  51.3 24.8 %collective-permute-start.4 = (bf16[512,1024]{1,0:T(8,128)(2,1)S(1)}, bf16[512,1024]{1,0:T(8,128)(2,1)S(1)}, u32[]{:S(2)}, u32[]{:S(2)}) collective-permute-start(bf16[512,1024]{1,0:T(8,128)(2,1)S(1)} %get-tuple-element.44.refs_1_.refs_2_), channel_id=1, source_target_pairs={{4,0},{8,4},{12,8},{14,12},{10,14},{6,10},{2,6},{0,2},{5,1},{9,5},... | collective-permute-start | bytes 3145736 | tf_op jit(solution)/shard_map/ppermute | solution.py:435
  51.3 24.7 %collective-permute-start.5 = (f32[5,16,512]{2,1,0:T(8,128)S(1)}, f32[5,16,512]{2,1,0:T(8,128)S(1)}, u32[]{:S(2)}, u32[]{:S(2)}) collective-permute-start(f32[5,16,512]{2,1,0:T(8,128)S(1)} %get-tuple-element.46), channel_id=1, source_target_pairs={{0,2},{2,0},{4,6},{6,4},{8,10},{10,8},{12,14},{14,12},{1,3},{3,1},... | collective-permute-start | bytes 491528 | tf_op jit(solution)/shard_map/ppermute | solution.py:442
  76.1 34.6 %collective-permute-start.6 = (bf16[512,1024]{1,0:T(8,128)(2,1)S(1)}, bf16[512,1024]{1,0:T(8,128)(2,1)S(1)}, u32[]{:S(2)}, u32[]{:S(2)}) collective-permute-start(bf16[512,1024]{1,0:T(8,128)(2,1)S(1)} %get-tuple-element.50.refs_0_.refs_3_), channel_id=1, source_target_pairs={{0,4},{4,8},{8,12},{12,14},{14,10},{10,6},{6,2},{2,0},{1,5},{5,9},... | collective-permute-start | bytes 3145736 | tf_op jit(solution)/shard_map/ppermute | solution.py:435
  76.2 34.6 %collective-permute-start.7 = (bf16[512,1024]{1,0:T(8,128)(2,1)S(1)}, bf16[512,1024]{1,0:T(8,128)(2,1)S(1)}, u32[]{:S(2)}, u32[]{:S(2)}) collective-permute-start(bf16[512,1024]{1,0:T(8,128)(2,1)S(1)} %get-tuple-element.51.refs_1_.refs_4_), channel_id=1, source_target_pairs={{4,0},{8,4},{12,8},{14,12},{10,14},{6,10},{2,6},{0,2},{5,1},{9,5},... | collective-permute-start | bytes 3145736 | tf_op jit(solution)/shard_map/ppermute | solution.py:435
  78.7 29.1 %collective-permute-start.10 = (f32[32,512]{1,0:T(8,128)S(1)}, f32[32,512]{1,0:T(8,128)S(1)}, u32[]{:S(2)}, u32[]{:S(2)}) collective-permute-start(f32[32,512]{1,0:T(8,128)S(1)} %get-tuple-element.54), channel_id=1, source_target_pairs={{0,12},{2,14},{4,8},{6,10},{8,4},{10,6},{12,0},{14,2},{1,13},{3,15... | collective-permute-start | bytes 196616 | tf_op jit(solution)/shard_map/ppermute | solution.py:442
  83.0 24.8 %collective-permute-start.8 = (f32[32,512]{1,0:T(8,128)S(1)}, f32[32,512]{1,0:T(8,128)S(1)}, u32[]{:S(2)}, u32[]{:S(2)}) collective-permute-start(f32[32,512]{1,0:T(8,128)S(1)} %get-tuple-element.52), channel_id=1, source_target_pairs={{0,4},{2,6},{4,0},{6,2},{8,12},{10,14},{12,8},{14,10},{1,5},{3,7},... | collective-permute-start | bytes 196616 | tf_op jit(solution)/shard_map/ppermute | solution.py:442
  83.0 26.4 %collective-permute-start.9 = (f32[32,512]{1,0:T(8,128)S(1)}, f32[32,512]{1,0:T(8,128)S(1)}, u32[]{:S(2)}, u32[]{:S(2)}) collective-permute-start(f32[32,512]{1,0:T(8,128)S(1)} %get-tuple-element.53), channel_id=1, source_target_pairs={{0,8},{2,10},{4,12},{6,14},{8,0},{10,2},{12,4},{14,6},{1,9},{3,11}... | collective-permute-start | bytes 196616 | tf_op jit(solution)/shard_map/ppermute | solution.py:442
  110.6 3.6 %collective-permute-start.13 = (f32[8,16,2048]{2,1,0:T(8,128)S(1)}, f32[8,16,2048]{2,1,0:T(8,128)S(1)}, u32[]{:S(2)}, u32[]{:S(2)}) collective-permute-start(f32[8,16,2048]{2,1,0:T(8,128)S(1)} %get-tuple-element.63), channel_id=1, source_target_pairs={{0,1},{1,0},{2,3},{3,2},{4,5},{5,4},{6,7},{7,6},{8,9},{9,8},{10,11... | collective-permute-start | bytes 3145736 | tf_op jit(solution)/shard_map/ppermute | solution.py:463
  110.8 19.3 %collective-permute-start.11 = (bf16[256,1024]{1,0:T(8,128)(2,1)S(1)}, bf16[256,1024]{1,0:T(8,128)(2,1)S(1)}, u32[]{:S(2)}, u32[]{:S(2)}) collective-permute-start(bf16[256,1024]{1,0:T(8,128)(2,1)S(1)} %get-tuple-element.58), channel_id=1, source_target_pairs={{0,4},{4,8},{8,12},{12,14},{14,10},{10,6},{6,2},{2,0},{1,5},{5,9},... | collective-permute-start | bytes 1572872 | tf_op jit(solution)/shard_map/ppermute | solution.py:435
  111.3 18.8 %collective-permute-start.12 = (bf16[256,1024]{1,0:T(8,128)(2,1)S(1)}, bf16[256,1024]{1,0:T(8,128)(2,1)S(1)}, u32[]{:S(2)}, u32[]{:S(2)}) collective-permute-start(bf16[256,1024]{1,0:T(8,128)(2,1)S(1)} %get-tuple-element.59), channel_id=1, source_target_pairs={{4,0},{8,4},{12,8},{14,12},{10,14},{6,10},{2,6},{0,2},{5,1},{9,5},... | collective-permute-start | bytes 1572872 | tf_op jit(solution)/shard_map/ppermute | solution.py:435
  114.3 16.9 %collective-permute-start.14 = (bf16[4,16,2048]{2,1,0:T(8,128)(2,1)S(1)}, bf16[4,16,2048]{2,1,0:T(8,128)(2,1)S(1)}, u32[]{:S(2)}, u32[]{:S(2)}) collective-permute-start(bf16[4,16,2048]{2,1,0:T(8,128)(2,1)S(1)} %get-tuple-element.72), channel_id=1, source_target_pairs={{0,2},{2,0},{4,6},{6,4},{8,10},{10,8},{12,14},{14,12},{1,3},{3,1},... | collective-permute-start | bytes 786440 | tf_op jit(solution)/shard_map/ppermute | solution.py:442
  131.2 19.1 %collective-permute-start.19 = (f32[16,4096]{1,0:T(8,128)S(1)}, f32[16,4096]{1,0:T(8,128)S(1)}, u32[]{:S(2)}, u32[]{:S(2)}) collective-permute-start(f32[16,4096]{1,0:T(8,128)S(1)} %get-tuple-element.78), channel_id=1, source_target_pairs={{0,1},{1,0},{2,3},{3,2},{4,5},{5,4},{6,7},{7,6},{8,9},{9,8},{10,11... | collective-permute-start | bytes 786440 | tf_op jit(solution)/shard_map/ppermute | solution.py:483
  131.3 17.8 %collective-permute-start.15 = (bf16[2,16,2048]{2,1,0:T(8,128)(2,1)S(1)}, bf16[2,16,2048]{2,1,0:T(8,128)(2,1)S(1)}, u32[]{:S(2)}, u32[]{:S(2)}) collective-permute-start(bf16[2,16,2048]{2,1,0:T(8,128)(2,1)S(1)} %get-tuple-element.73), channel_id=1, source_target_pairs={{0,0},{1,4},{2,2},{3,6},{4,8},{5,12},{6,10},{7,14},{8,1},{9,5},{10... | collective-permute-start | bytes 393224 | tf_op jit(solution)/shard_map/ppermute | solution.py:480
  132.0 17.2 %collective-permute-start.16 = (bf16[2,16,2048]{2,1,0:T(8,128)(2,1)S(1)}, bf16[2,16,2048]{2,1,0:T(8,128)(2,1)S(1)}, u32[]{:S(2)}, u32[]{:S(2)}) collective-permute-start(bf16[2,16,2048]{2,1,0:T(8,128)(2,1)S(1)} %get-tuple-element.74), channel_id=1, source_target_pairs={{0,4},{1,0},{2,6},{3,2},{4,12},{5,8},{6,14},{7,10},{8,5},{9,1},{10... | collective-permute-start | bytes 393224 | tf_op jit(solution)/shard_map/ppermute | solution.py:480
  134.1 15.0 %collective-permute-start.17 = (bf16[2,16,2048]{2,1,0:T(8,128)(2,1)S(1)}, bf16[2,16,2048]{2,1,0:T(8,128)(2,1)S(1)}, u32[]{:S(2)}, u32[]{:S(2)}) collective-permute-start(bf16[2,16,2048]{2,1,0:T(8,128)(2,1)S(1)} %get-tuple-element.75), channel_id=1, source_target_pairs={{0,8},{1,12},{2,10},{3,14},{4,0},{5,4},{6,2},{7,6},{8,9},{9,13},{1... | collective-permute-start | bytes 393224 | tf_op jit(solution)/shard_map/ppermute | solution.py:480
  136.4 12.8 %collective-permute-start.18 = (bf16[2,16,2048]{2,1,0:T(8,128)(2,1)S(1)}, bf16[2,16,2048]{2,1,0:T(8,128)(2,1)S(1)}, u32[]{:S(2)}, u32[]{:S(2)}) collective-permute-start(bf16[2,16,2048]{2,1,0:T(8,128)(2,1)S(1)} %get-tuple-element.76), channel_id=1, source_target_pairs={{0,12},{1,8},{2,14},{3,10},{4,4},{5,0},{6,6},{7,2},{8,13},{9,9},{1... | collective-permute-start | bytes 393224 | tf_op jit(solution)/shard_map/ppermute | solution.py:480
where the time goes:
time: 152 us; the launch traced here: 151 us
  Pallas kernels  71 us (47%)
  waiting for transfers between devices  38.9 us (26%)
  starting transfers between devices  33.5 us (22%)
  local copies, waits for them, and re-layouts  6.05 us (4%)
    pallas_call x5, Pallas kernels, base_step(): pl.pallas_call(functools.partial(base_kernel, nc, first, last, low, wide,...  62.8 us
    ppermute x5, waiting for transfers between devices, xor(): return lax.ppermute(x, 'tensor', [(j, j ^ r) for j in range(n)])  20.8 us
    all_to_all x1, waiting for transfers between devices, exchange(): return lax.all_to_all(x, 'tensor', split_axis=0, concat_axis=0, tiled=True)  16.7 us
    ppermute x4, starting transfers between devices, small_ring(): routed.append(lax.ppermute(piece, ('tensor', 'dp'), hops))  7.9 us
    ppermute x4, starting transfers between devices, ring_step(): lax.ppermute(right, 'tensor', forth)  7.54 us
    all_to_all x1, starting transfers between devices, exchange(): return lax.all_to_all(x, 'tensor', split_axis=0, concat_axis=0, tiled=True)  7.28 us
    ppermute x5, starting transfers between devices, xor(): return lax.ppermute(x, 'tensor', [(j, j ^ r) for j in range(n)])  6.43 us
    unnamed x17, local copies, waits for them, and re-layouts  4.67 us
  transfers between devices with their start and end apart: 21, of which 5 were waited for; matrix products, arithmetic and copies ran while one was open for 1% of the time, Pallas kernels for 46%

commit v1 on v0

--- a/solution.py
+++ b/solution.py
@@ -27,17 +27,17 @@
     return lax.dot_general(a, b, (((ca,), (cb,)), ((), ())), preferred_element_type=f32)
 
 
-def base_kernel(nc, first, last, low, wide, rows, whole_in, whole_out, ids, *refs):
+def base_kernel(nc, first, last, low, wide, rows, ids, *refs):
     refs = list(refs)
     c_refs, q_refs, s_refs = refs[:nc], refs[nc : 2 * nc], refs[2 * nc : 3 * nc]
     refs = refs[3 * nc :]
     acc_ref = None if first else refs.pop(0)
     r_ref, d_ref = (refs.pop(0), refs.pop(0)) if low else (None, None)
-    rin_ref = refs.pop(0) if wide else None
+    rin_ref, had_ref = (refs.pop(0), refs.pop(0)) if wide else (None, None)
     cd, sd = refs[-2:]
     up_ref = refs[-3] if wide else None
     out_ref, token_ref = refs[-5:-3] if wide else refs[-4:-2]
-    width = cd.shape[2]
+    width = cd.shape[1]
     step = pl.program_id(0)
 
     @pl.when(step == 0)
@@ -46,13 +46,15 @@
         col = lax.broadcasted_iota(jnp.int32, (256, 256), 1)
         perm = (row == 2 * (col % 128) + col // 128).astype(f32).astype(bf16)
         token_ref[...] = jnp.zeros_like(token_ref)
+        if wide:
+            up_ref[...] = had_ref[...]
         for c in range(nc):
             if wide:
                 at = pl.ds(pl.multiple_of(ids[c] * width, width), width)
                 up_ref[:, at] = 2.0 * xdot(rin_ref[...], c_refs[c][...], 1, 0)
             for b in range(width // 256):
                 at = slice(b * 256, b * 256 + 256)
-                cd[c, :, at] = xdot(c_refs[c][:, at], perm, 1, 0).astype(bf16)
+                cd[c, at] = xdot(perm, c_refs[c][:, at], 0, 1).astype(bf16)
                 sd[c, :, at] = xdot(s_refs[c][:, at], perm, 1, 0)
 
     total = None
@@ -70,20 +72,20 @@
                 ).reshape(rows, 128)
                 parts.append((code - 8).astype(bf16) * scale)
         weight = jnp.concatenate(parts, axis=1)
-        term = xdot(cd[c], weight, 1, 1)
+        term = jnp.dot(weight, cd[c], preferred_element_type=f32)
         total = term if total is None else total + term
-    cols = pl.ds(pl.multiple_of(step * rows, rows), rows)
+    at = pl.ds(pl.multiple_of(step * rows, rows), rows)
     if acc_ref is not None:
-        total = total + (acc_ref[:, cols] if whole_in else acc_ref[...])
+        total = total + acc_ref[at, :]
     if low:
-        total = total + (2.0 * xdot(r_ref[...], d_ref[...], 1, 0)).astype(bf16).astype(f32)
-    if whole_out:
-        out_ref[:, cols] = total
+        total = total + (2.0 * xdot(d_ref[...], r_ref[...], 0, 0)).astype(bf16).astype(f32)
+    if last:
+        out_ref[...] = total.T.astype(out_ref.dtype)
     else:
-        out_ref[...] = total.astype(out_ref.dtype)
-
-
-def base_step(ids, chunks, q, s, acc=None, adapter=None, up=None, last=False, after=(), rows=1024, whole=(True, True), limit=24):
+        out_ref[at, :] = total
+
+
+def base_step(ids, chunks, q, s, acc=None, adapter=None, up=None, last=False, after=(), rows=1024):
     nc = len(chunks)
     tok, width = chunks[0].shape
     hidden = q.shape[0]
@@ -97,24 +99,22 @@
     in_specs += [pl.BlockSpec((groups, width), lambda i, ids, c=c: (0, ids[c])) for c in range(nc)]
     args = list(chunks) + [q] * nc + [s] * nc
     aliases = {}
-    whole_in, whole_out = whole[0], whole[1] and not last
-    block = pl.BlockSpec((tok, rows), lambda i, ids: (0, i))
     if not first:
-        if whole_in == whole_out and not last:
+        if not last:
             aliases = {1 + len(args): 0}
-        in_specs.append(vm if whole_in else block)
+        in_specs.append(vm)
         args.append(acc)
     if low:
-        ranks = adapter[0].shape[1]
-        in_specs.append(pl.BlockSpec((tok, ranks), lambda i, ids: (0, 0)))
+        ranks = adapter[0].shape[0]
+        in_specs.append(vm)
         in_specs.append(pl.BlockSpec((ranks, rows), lambda i, ids: (0, i)))
         args += list(adapter)
     out_specs = [
-        vm if whole_out else block,
+        pl.BlockSpec((tok, rows), lambda i, ids: (0, i)) if last else vm,
         pl.BlockSpec((8, 128), lambda i, ids: (0, 0)),
     ]
     out_shape = [
-        jax.ShapeDtypeStruct((tok, hidden), bf16 if last else f32),
+        jax.ShapeDtypeStruct((tok, hidden), bf16) if last else jax.ShapeDtypeStruct((hidden, tok), f32),
         jax.ShapeDtypeStruct((8, 128), f32),
     ]
     if wide:
@@ -126,18 +126,18 @@
     in_specs += [pl.BlockSpec(memory_space=pl.ANY)] * len(after)
     args += list(after)
     return pl.pallas_call(
-        functools.partial(base_kernel, nc, first, last, low, wide, rows, whole_in, whole_out),
+        functools.partial(base_kernel, nc, first, last, low, wide, rows),
         grid_spec=pltpu.PrefetchScalarGridSpec(
             num_scalar_prefetch=1,
             grid=(hidden // rows,),
             in_specs=in_specs,
             out_specs=out_specs,
-            scratch_shapes=[pltpu.VMEM((nc, tok, width), bf16), pltpu.VMEM((nc, groups, width), f32)],
+            scratch_shapes=[pltpu.VMEM((nc, width, tok), bf16), pltpu.VMEM((nc, groups, width), f32)],
         ),
         out_shape=out_shape,
         input_output_aliases=aliases,
-        compiler_params=params(limit),
-        cost_estimate=cost(1000, 1000),
+        compiler_params=params(24),
+        cost_estimate=cost(2 * nc * tok * hidden * width, 25000000 * nc),
     )(ids, *args)
 
 
@@ -166,7 +166,7 @@
         functools.partial(pack_kernel, n),
         out_shape=jax.ShapeDtypeStruct((n, rank, cols), bf16),
         compiler_params=params(16),
-        cost_estimate=cost(1000, 1000),
+        cost_estimate=cost(1000, 4000000),
     )(down, up)
 
 
@@ -204,7 +204,7 @@
         out_shape=[part, part, jax.ShapeDtypeStruct((n * rank, hidden), bf16)],
         scratch_shapes=[pltpu.VMEM((n * rank, cot.shape[1]), bf16)],
         compiler_params=params(16),
-        cost_estimate=cost(1000, 1000),
+        cost_estimate=cost(1000, 4000000),
     )(owner, job, act, cot, own, got, after)
 
 
@@ -226,7 +226,7 @@
         out_specs=[VM] * (n // 2),
         out_shape=[jax.ShapeDtypeStruct((2 * rank, tok), f32)] * (n // 2),
         compiler_params=params(16),
-        cost_estimate=cost(1000, 1000),
+        cost_estimate=cost(1000, 4000000),
     )(keep, got, after)
 
 
@@ -240,8 +240,8 @@
     rin_ref[...] = jnp.where(slot == me, total[:rank], 0.0).astype(bf16)
     rout = total[rank:].astype(bf16).astype(f32)
     spread = jnp.concatenate([jnp.where(slot == r, rout, 0.0) for r in range(n)], axis=0)
-    r_ref[...] = spread.T.astype(bf16)
     left = spread.astype(bf16)
+    r_ref[...] = left
     half = act_ref.shape[1] // 2
     for ref, which in ((send_ref, 1 - core), (keep_ref, core)):
         cols = pl.ds(pl.multiple_of(which * half, half), half)
@@ -258,12 +258,12 @@
         out_specs=[VM] * 4,
         out_shape=[
             jax.ShapeDtypeStruct((rank, tok), bf16),
-            jax.ShapeDtypeStruct((tok, n * rank), bf16),
+            jax.ShapeDtypeStruct((n * rank, tok), bf16),
             half,
             half,
         ],
         compiler_params=params(16),
-        cost_estimate=cost(1000, 1000),
+        cost_estimate=cost(1000, 4000000),
     )(owner, job, act, *parts, after)
 
 
@@ -282,7 +282,7 @@
         out_specs=[VM, VM],
         out_shape=[jax.ShapeDtypeStruct((n // 2, rank, cols), bf16)] * 2,
         compiler_params=params(16),
-        cost_estimate=cost(1000, 1000),
+        cost_estimate=cost(1000, 4000000),
     )(keep, got, after)
 
 
@@ -302,7 +302,7 @@
         out_specs=[VM] * rounds,
         out_shape=[jax.ShapeDtypeStruct((2, rank, cols), bf16)] * rounds,
         compiler_params=params(16),
-        cost_estimate=cost(1000, 1000),
+        cost_estimate=cost(1000, 4000000),
     )(own, got, after)
 
 
@@ -326,7 +326,7 @@
         in_specs=[VM] * len(parts) + [ANY],
         out_shape=jax.ShapeDtypeStruct((1, rank, 2 * len(parts) * cols), f32),
         compiler_params=params(16),
-        cost_estimate=cost(1000, 1000),
+        cost_estimate=cost(1000, 4000000),
     )(*parts, after)
 
 
@@ -334,12 +334,12 @@
     pass
 
 
-def tie(arrays, after, spec):
+def tie(arrays, after):
     n = len(arrays)
     return pl.pallas_call(
         tie_kernel,
-        in_specs=[spec] * n + [ANY],
-        out_specs=[spec] * n,
+        in_specs=[ANY] * (n + 1),
+        out_specs=[ANY] * n,
         out_shape=[jax.ShapeDtypeStruct(x.shape, x.dtype) for x in arrays],
         input_output_aliases={i: i for i in range(n)},
         compiler_params=params(16),
@@ -361,7 +361,7 @@
         out_specs=[VM, VM],
         out_shape=[half, half],
         compiler_params=params(16),
-        cost_estimate=cost(1000, 1000),
+        cost_estimate=cost(1000, 4000000),
     )(right, left, after)
 
 
@@ -383,7 +383,7 @@
         out_specs=vm,
         out_shape=jax.ShapeDtypeStruct((rin.shape[0], CHUNKS * width), f32),
         compiler_params=params(16),
-        cost_estimate=cost(1000, 1000),
+        cost_estimate=cost(1000, 4000000),
     )(ids, rin, *chunks, after)
 
 
@@ -411,7 +411,7 @@
         out_specs=[vm, vm],
         out_shape=[half, half],
         compiler_params=params(16),
-        cost_estimate=cost(1000, 1000),
+        cost_estimate=cost(1000, 4000000),
     )(ids, rin, chunk, up, after)
 
 
@@ -444,25 +444,27 @@
     pairs = [ids[2 * h - 1 : 2 * h + 1] for h in range(1, n // 2)]
 
     right1, left1 = ring_step(cot, cot)
-    pieces = exchange(pack(down, up, n))
+    sent = pack(down, up, n)
+    pieces = exchange(sent)
+    acc, token = base_step(ids[:1], [cot], q, scales, after=[sent])
+
+    right1, left1 = tie((right1, left1), token)
+    right2, left2 = ring_step(right1, left1)
+    acc, token = base_step(pairs[0], [right1, left1], q, scales, acc)
+    (pieces,) = tie((pieces,), token)
     other = lax.ppermute(pieces, "dp", swap)
-    acc, token = base_step(ids[:1], [cot], q, scales, after=[pieces])
     keep, send, down_cols = ranks(owner, job_row, act, cot, pieces, other, token)
     got = xor(send, 1)
 
-    right1, left1 = tie((right1, left1), down_cols, VM)
-    right2, left2 = ring_step(right1, left1)
-    acc, token = base_step(pairs[0], [right1, left1], q, scales, acc, after=[down_cols])
-    mixed = mix(n, keep, got, token)
+    right2, left2 = tie((right2, left2), down_cols)
+    right3, left3 = ring_step(right2, left2)
+    mixed = mix(n, keep, got, right2)
     parts = [mixed[0]] + [xor(mixed[r], 2 * r) for r in range(1, n // 2)]
-
-    right2, left2 = tie((right2, left2), mixed[0], VM)
-    right3, left3 = ring_step(right2, left2)
     acc, token = base_step(pairs[1], [right2, left2], q, scales, acc, after=[mixed[0]])
+
+    halves = ring_step(*cut(right3, left3, token))
     rin, spread, keep, send = grads(owner, job_row, act, parts, token)
     got = lax.ppermute(send, "dp", swap)
-
-    halves = ring_step(*cut(right3, left3, rin))
     grad_up = up_step(ids[:5], rin, [cot, right1, left1, right2, left2], rin)
     own, send = split(keep, got, grad_up)
     got = xor(send, 1)
@@ -478,7 +480,7 @@
                     to = ((z % 2) * 2 + core) ^ r
                     hops.append((z * 4 + y * 2 + core, to * 4 + y * 2 + z // 2))
         routed.append(lax.ppermute(piece, ("tensor", "dp"), hops))
-    last = jnp.concatenate(tie(halves, token, VM), axis=0)
+    last = jnp.concatenate(tie(halves, token), axis=0)
     keep, send = up_last(ids[n - 1 :], rin, last, grad_up, token)
     other = lax.ppermute(send, "dp", swap)
     grad_input, token = base_step(ids[n - 1 :], [last], q, scales, acc, last=True, after=[keep])
@@ -516,7 +518,7 @@
     for c in range(2, CHUNKS - 2, 2):
         acc, _ = base_step(ids[c : c + 2], chunks[c : c + 2], q, scales, acc)
     grad_input, _ = base_step(
-        ids[CHUNKS - 2 :], chunks[CHUNKS - 2 :], q, scales, acc, (spread, down_cols), last=True
+        ids[CHUNKS - 2 :], chunks[CHUNKS - 2 :], q, scales, acc, (spread.T, down_cols), last=True
     )
     return grad_input, grad_a, grad_b
 

time: 152 us -> 141 us (0.928)
  waiting for transfers between devices: 38.9 us -> 14.4 us
  local copies, waits for them, and re-layouts: 6.05 us -> 13.1 us
  starting transfers between devices: 33.5 us -> 38.7 us
  Pallas kernels: 71 us -> 72.6 us
    all_to_all x1, waiting for transfers between devices: 16.7 us -> 0.01 us  [exchange(): return lax.all_to_all(x, 'tensor', split_axis=0, concat_axis=0, tiled=True)]
    ppermute x5, waiting for transfers between devices: 20.8 us -> 4.78 us  [xor(): return lax.ppermute(x, 'tensor', [(j, j ^ r) for j in range(n)])]
    unnamed x17 -> x27, local copies, waits for them, and re-layouts: 4.67 us -> 11.7 us
    ppermute x4, starting transfers between devices: 7.54 us -> 11.6 us  [ring_step(): lax.ppermute(right, 'tensor', forth)]
    ppermute x4, waiting for transfers between devices: 1.36 us -> 4.58 us  [ring_step(): lax.ppermute(left, 'tensor', back)]
    ppermute x4, waiting for transfers between devices: 0.01 us -> 2.75 us  [ring_step(): lax.ppermute(right, 'tensor', forth)]
    ppermute x1, waiting for transfers between devices: 0.01 us -> 2.3 us  [small_ring(): other = lax.ppermute(pieces, 'dp', swap)]
    ppermute x5, starting transfers between devices: 6.43 us -> 8.69 us  [xor(): return lax.ppermute(x, 'tensor', [(j, j ^ r) for j in range(n)])]
  transfers between devices with their start and end apart: 21 -> 21, of which waited for: 5 -> 9; matrix products, arithmetic and copies ran while one was open for 1% -> 1% of each run, Pallas kernels for 46% -> 52%
where the time goes in v1:
time: 141 us; the launch traced here: 140 us
  Pallas kernels  72.6 us (51%)
  starting transfers between devices  38.7 us (27%)
  waiting for transfers between devices  14.4 us (10%)
  local copies, waits for them, and re-layouts  13.1 us (9%)
    pallas_call x5, Pallas kernels, base_step(): pl.pallas_call(functools.partial(base_kernel, nc, first, last, low, wide,...  63 us
    unnamed x27, local copies, waits for them, and re-layouts  11.7 us
    ppermute x4, starting transfers between devices, ring_step(): lax.ppermute(right, 'tensor', forth)  11.6 us
    ppermute x4, starting transfers between devices, small_ring(): routed.append(lax.ppermute(piece, ('tensor', 'dp'), hops))  9.82 us
    ppermute x5, starting transfers between devices, xor(): return lax.ppermute(x, 'tensor', [(j, j ^ r) for j in range(n)])  8.69 us
    all_to_all x1, starting transfers between devices, exchange(): return lax.all_to_all(x, 'tensor', split_axis=0, concat_axis=0, tiled=True)  6.27 us
    ppermute x5, waiting for transfers between devices, xor(): return lax.ppermute(x, 'tensor', [(j, j ^ r) for j in range(n)])  4.78 us
    ppermute x4, waiting for transfers between devices, ring_step(): lax.ppermute(left, 'tensor', back)  4.58 us
  transfers between devices with their start and end apart: 21, of which 9 were waited for; matrix products, arithmetic and copies ran while one was open for 1% of the time, Pallas kernels for 52%

profile of v1, /device:TPU:0, one launch (start us, length us, event | category | flops | bytes accessed | tf_op | source)
XLA Modules:
  0.0 140.4 jit_solution(6633878498466353423)
XLA Ops:
  0.6 3.1 %collective-permute-start = (bf16[512,1024]{1,0:T(8,128)(2,1)}, bf16[512,1024]{1,0:T(8,128)(2,1)}, u32[]{:S(2)}, u32[]{:S(2)}) collective-permute-start(bf16[512,1024]{1,0:T(8,128)(2,1)} %refs_0_.3), channel_id=1, source_target_pairs={{0,4},{4,8},{8,12},{12,14},{14,10},{10,6},{6,2},{2,0},{1,5},{5,9},... | collective-permute-start | bytes 3145736 | tf_op jit(solution)/shard_map/ppermute | solution.py:435
  3.7 1.2 copy-done.9
  6.8 6.3 %all-to-all-start = ((bf16[8,16,2560]{2,1,0:T(8,128)(2,1)}), bf16[8,16,2560]{2,1,0:T(8,128)(2,1)}, u32[]{:S(2)}, u32[]{:S(2)}) async-start(bf16[8,16,2560]{2,1,0:T(8,128)(2,1)} %shard_map.112.refs_3_), calls=%async_computation | async-start | bytes 1310720 | tf_op jit(solution)/shard_map/all_to_all | solution.py:438
  14.4 1.2 copy-done.2
  15.6 1.2 copy-done.6
  16.8 8.4 %shard_map.113 = (f32[4096,512]{1,0:T(8,128)S(1)}, f32[8,128]{1,0:T(8,128)S(1)}) custom-call(s32[1]{0:T(128)} %bitcast.1.ids, bf16[512,1024]{1,0:T(8,128)(2,1)S(1)} %copy-done.6, s32[4096,4096]{1,0:T(8,128)} %refs_1_.3, bf16[64,8192]{1,0:T(8,128)(2,1)S(1)} %copy-done.2, bf16[8,16,2560]{2,1,0:T(8,128)(2,1)} %shard_map.112.refs_3_), custom_call_target="tpu_custom_call" | custom-call | flops 4294967296 | bytes 25000000 | tf_op jit(solution)/shard_map/pallas_call | solution.py:128
  25.2 2.7 %collective-permute-done.refs_0_ = bf16[512,1024]{1,0:T(8,128)(2,1)} collective-permute-done((bf16[512,1024]{1,0:T(8,128)(2,1)}, bf16[512,1024]{1,0:T(8,128)(2,1)}, u32[]{:S(2)}, u32[]{:S(2)}) %collective-permute-start) | collective-permute-done | bytes 1048608 | tf_op jit(solution)/shard_map/ppermute | solution.py:435
  28.0 2.1 %collective-permute-done.1.refs_1_ = bf16[512,1024]{1,0:T(8,128)(2,1)} collective-permute-done((bf16[512,1024]{1,0:T(8,128)(2,1)}, bf16[512,1024]{1,0:T(8,128)(2,1)}, u32[]{:S(2)}, u32[]{:S(2)}) %collective-permute-start.1) | collective-permute-done | bytes 1048608 | tf_op jit(solution)/shard_map/ppermute | solution.py:435
  30.1 1.7 %collective-permute-start.2 = (bf16[512,1024]{1,0:T(8,128)(2,1)}, bf16[512,1024]{1,0:T(8,128)(2,1)S(1)}, u32[]{:S(2)}, u32[]{:S(2)}) collective-permute-start(bf16[512,1024]{1,0:T(8,128)(2,1)} %get-tuple-element.42.refs_0_.refs_1_), channel_id=1, source_target_pairs={{0,4},{4,8},{8,12},{12,14},{14,10},{10,6},{6,2},{2,0},{1,5},{5,9},... | collective-permute-start | bytes 3145736 | tf_op jit(solution)/shard_map/ppermute | solution.py:435
  32.1 14.6 %shard_map.115 = (f32[4096,512]{1,0:T(8,128)S(1)}, f32[8,128]{1,0:T(8,128)S(1)}) custom-call(s32[2]{0:T(128)S(1)} %get-tuple-element.81.ids, bf16[512,1024]{1,0:T(8,128)(2,1)} %get-tuple-element.42.refs_0_.refs_1_, bf16[512,1024]{1,0:T(8,128)(2,1)} %get-tuple-element.43.refs_1_.refs_2_, s32[4096,4096]{1,0:T(8,128)} %refs_1_.3, ...), custom_call_target="tpu_custom_call", output_to_operand_aliasing={{0}: (7, {})} | custom-call | flops 8589934592 | bytes 50000000 | tf_op jit(solution)/shard_map/pallas_call | solution.py:128
  46.7 3.3 %copy-done = f32[4096,512]{1,0:T(8,128)} copy-done((f32[4096,512]{1,0:T(8,128)}, f32[4096,512]{1,0:T(8,128)S(1)}, u32[]{:S(2)}) %copy-start) | copy-done | bytes 8388632
  50.1 2.3 %collective-permute-done.4.got_ref = bf16[8,16,2560]{2,1,0:T(8,128)(2,1)S(1)} collective-permute-done((bf16[8,16,2560]{2,1,0:T(8,128)(2,1)}, bf16[8,16,2560]{2,1,0:T(8,128)(2,1)S(1)}, u32[]{:S(2)}, u32[]{:S(2)}) %collective-permute-start.4) | collective-permute-done | bytes 655392 | tf_op jit(solution)/shard_map/ppermute | solution.py:455
  52.4 2.5 %copy-done.4 = bf16[512,4096]{1,0:T(8,128)(2,1)S(1)} copy-done((bf16[512,4096]{1,0:T(8,128)(2,1)S(1)}, bf16[512,4096]{1,0:T(8,128)(2,1)}, u32[]{:S(2)}) %copy-start.4) | copy-done | bytes 4194328
  54.9 1.2 copy-done.7
  56.1 3.0 %shard_map.117 = (f32[5,16,512]{2,1,0:T(8,128)S(1)}, f32[5,16,512]{2,1,0:T(8,128)S(1)}, bf16[128,4096]{1,0:T(8,128)(2,1)S(1)}) custom-call(s32[8]{0:T(128)S(1)} %copy-done.12, s32[1,512]{1,0:T(1,128)S(1)} %bitcast.17, bf16[512,4096]{1,0:T(8,128)(2,1)S(1)} %copy-done.4, bf16[512,1024]{1,0:T(8,128)(2,1)S(1)} %copy-done.7, ...), custom_call_target="tpu_custom_call" | custom-call | flops 1000 | bytes 4000000 | tf_op jit(solution)/shard_map/pallas_call | solution.py:200
  59.2 3.4 %collective-permute-start.7 = (f32[5,16,512]{2,1,0:T(8,128)S(1)}, f32[5,16,512]{2,1,0:T(8,128)S(1)}, u32[]{:S(2)}, u32[]{:S(2)}) collective-permute-start(f32[5,16,512]{2,1,0:T(8,128)S(1)} %get-tuple-element.51), channel_id=1, source_target_pairs={{0,2},{2,0},{4,6},{6,4},{8,10},{10,8},{12,14},{14,12},{1,3},{3,1},... | collective-permute-start | bytes 491528 | tf_op jit(solution)/shard_map/ppermute | solution.py:442
  62.5 4.1 %collective-permute-start.5 = (bf16[512,1024]{1,0:T(8,128)(2,1)S(1)}, bf16[512,1024]{1,0:T(8,128)(2,1)S(1)}, u32[]{:S(2)}, u32[]{:S(2)}) collective-permute-start(bf16[512,1024]{1,0:T(8,128)(2,1)S(1)} %get-tuple-element.47.after.refs_0_.refs_3_), channel_id=1, source_target_pairs={{0,4},{4,8},{8,12},{12,14},{14,10},{10,6},{6,2},{2,0},{1,5},{5,9},... | collective-permute-start | bytes 3145736 | tf_op jit(solution)/shard_map/ppermute | solution.py:435
  67.6 1.9 %collective-permute-start.10 = (f32[32,512]{1,0:T(8,128)S(1)}, f32[32,512]{1,0:T(8,128)S(1)}, u32[]{:S(2)}, u32[]{:S(2)}) collective-permute-start(f32[32,512]{1,0:T(8,128)S(1)} %get-tuple-element.57), channel_id=1, source_target_pairs={{0,4},{2,6},{4,0},{6,2},{8,12},{10,14},{12,8},{14,10},{1,5},{3,7},... | collective-permute-start | bytes 196616 | tf_op jit(solution)/shard_map/ppermute | solution.py:442
  69.5 1.9 %collective-permute-start.11 = (f32[32,512]{1,0:T(8,128)S(1)}, f32[32,512]{1,0:T(8,128)S(1)}, u32[]{:S(2)}, u32[]{:S(2)}) collective-permute-start(f32[32,512]{1,0:T(8,128)S(1)} %get-tuple-element.58), channel_id=1, source_target_pairs={{0,8},{2,10},{4,12},{6,14},{8,0},{10,2},{12,4},{14,6},{1,9},{3,11}... | collective-permute-start | bytes 196616 | tf_op jit(solution)/shard_map/ppermute | solution.py:442
  72.4 1.7 %collective-permute-start.6 = (bf16[512,1024]{1,0:T(8,128)(2,1)S(1)}, bf16[512,1024]{1,0:T(8,128)(2,1)S(1)}, u32[]{:S(2)}, u32[]{:S(2)}) collective-permute-start(bf16[512,1024]{1,0:T(8,128)(2,1)S(1)} %get-tuple-element.48.refs_1_.refs_4_), channel_id=1, source_target_pairs={{4,0},{8,4},{12,8},{14,12},{10,14},{6,10},{2,6},{0,2},{5,1},{9,5},... | collective-permute-start | bytes 3145736 | tf_op jit(solution)/shard_map/ppermute | solution.py:435
  74.1 14.3 %shard_map.120 = (f32[4096,512]{1,0:T(8,128)S(1)}, f32[8,128]{1,0:T(8,128)S(1)}) custom-call(s32[2]{0:T(128)S(1)} %get-tuple-element.80.ids, bf16[512,1024]{1,0:T(8,128)(2,1)S(1)} %get-tuple-element.47.after.refs_0_.refs_3_, bf16[512,1024]{1,0:T(8,128)(2,1)S(1)} %get-tuple-element.48.refs_1_.refs_4_, ...), custom_call_target="tpu_custom_call", output_to_operand_aliasing={{0}: (7, {})} | custom-call | flops 8589934592 | bytes 50000000 | tf_op jit(solution)/shard_map/pallas_call | solution.py:128
  88.4 2.3 %collective-permute-done.10.refs_1_ = f32[32,512]{1,0:T(8,128)S(1)} collective-permute-done((f32[32,512]{1,0:T(8,128)S(1)}, f32[32,512]{1,0:T(8,128)S(1)}, u32[]{:S(2)}, u32[]{:S(2)}) %collective-permute-start.10) | collective-permute-done | bytes 65568 | tf_op jit(solution)/shard_map/ppermute | solution.py:442
  92.1 1.3 shard_map.122
  93.5 2.3 %shard_map.123.after.refs_10_ = f32[16,8192]{1,0:T(8,128)S(1)} custom-call(s32[5]{0:T(128)S(1)} %slice_bitcast_fusion.ids, bf16[16,512]{1,0:T(8,128)(2,1)S(1)} %get-tuple-element.61.rin_ref.refs_5_.refs_9_, bf16[512,1024]{1,0:T(8,128)(2,1)S(1)} %copy-done.8, bf16[512,1024]{1,0:T(8,128)(2,1)} %get-tuple-element.42.refs_0_.refs_1_, ...), custom_call_target="tpu_custom_call" | custom-call | flops 1000 | bytes 4000000 | tf_op jit(solution)/shard_map/pallas_call | solution.py:380
  95.8 2.4 %collective-permute-done.6.left_ref.refs_1_ = bf16[512,1024]{1,0:T(8,128)(2,1)S(1)} collective-permute-done((bf16[512,1024]{1,0:T(8,128)(2,1)S(1)}, bf16[512,1024]{1,0:T(8,128)(2,1)S(1)}, u32[]{:S(2)}, u32[]{:S(2)}) %collective-permute-start.6) | collective-permute-done | bytes 1048608 | tf_op jit(solution)/shard_map/ppermute | solution.py:435
  98.3 2.7 %collective-permute-start.8 = (bf16[256,1024]{1,0:T(8,128)(2,1)S(1)}, bf16[256,1024]{1,0:T(8,128)(2,1)S(1)}, u32[]{:S(2)}, u32[]{:S(2)}) collective-permute-start(bf16[256,1024]{1,0:T(8,128)(2,1)S(1)} %get-tuple-element.54), channel_id=1, source_target_pairs={{0,4},{4,8},{8,12},{12,14},{14,10},{10,6},{6,2},{2,0},{1,5},{5,9},... | collective-permute-start | bytes 1572872 | tf_op jit(solution)/shard_map/ppermute | solution.py:435
  101.7 15.7 %shard_map.125 = (f32[4096,512]{1,0:T(8,128)S(1)}, f32[8,128]{1,0:T(8,128)S(1)}, f32[16,8192]{1,0:T(8,128)S(1)}) custom-call(s32[2]{0:T(128)S(1)} %get-tuple-element.79.ids, bf16[512,1024]{1,0:T(8,128)(2,1)S(1)} %collective-permute-done.5.right_ref.refs_0_, ...), custom_call_target="tpu_custom_call", output_to_operand_aliasing={{0}: (7, {}), {2}: (11, {})} | custom-call | flops 8589934592 | bytes 50000000 | tf_op jit(solution)/shard_map/pallas_call | solution.py:128
  118.3 5.6 %collective-permute-start.16 = (bf16[2,16,2048]{2,1,0:T(8,128)(2,1)S(1)}, bf16[2,16,2048]{2,1,0:T(8,128)(2,1)S(1)}, u32[]{:S(2)}, u32[]{:S(2)}) collective-permute-start(bf16[2,16,2048]{2,1,0:T(8,128)(2,1)S(1)} %get-tuple-element.74), channel_id=1, source_target_pairs={{0,4},{1,0},{2,6},{3,2},{4,12},{5,8},{6,14},{7,10},{8,5},{9,1},{10... | collective-permute-start | bytes 393224 | tf_op jit(solution)/shard_map/ppermute | solution.py:482
  123.9 1.1 collective-permute-start.17
  125.0 2.4 %collective-permute-start.18 = (bf16[2,16,2048]{2,1,0:T(8,128)(2,1)S(1)}, bf16[2,16,2048]{2,1,0:T(8,128)(2,1)S(1)}, u32[]{:S(2)}, u32[]{:S(2)}) collective-permute-start(bf16[2,16,2048]{2,1,0:T(8,128)(2,1)S(1)} %get-tuple-element.76), channel_id=1, source_target_pairs={{0,12},{1,8},{2,14},{3,10},{4,4},{5,0},{6,6},{7,2},{8,13},{9,9},{1... | collective-permute-start | bytes 393224 | tf_op jit(solution)/shard_map/ppermute | solution.py:482
  128.5 10.1 %shard_map.128 = (bf16[512,4096]{1,0:T(8,128)(2,1)}, f32[8,128]{1,0:T(8,128)S(1)}) custom-call(s32[1]{0:T(128)} %bitcast.ids, bf16[512,1024]{1,0:T(8,128)(2,1)S(1)} %constant_dynamic-update-slice_fusion.chunk_ref.refs_0_, s32[4096,4096]{1,0:T(8,128)} %refs_1_.3, bf16[64,8192]{1,0:T(8,128)(2,1)S(1)} %copy-done.3, f32[4096,512]{1,0:T(8,128)S(1)} %get-tuple-element.68.refs_3_, ...), custom_call_target="tpu_custom_call" | custom-call | flops 4294967296 | bytes 25000000 | tf_op jit(solution)/shard_map/pallas_call | solution.py:128
  138.6 1.1 shard_map.130
  (62 shorter events, 10.4 us)
Async XLA Ops:
  0.6 27.3 %collective-permute-start = (bf16[512,1024]{1,0:T(8,128)(2,1)}, bf16[512,1024]{1,0:T(8,128)(2,1)}, u32[]{:S(2)}, u32[]{:S(2)}) collective-permute-start(bf16[512,1024]{1,0:T(8,128)(2,1)} %refs_0_.3), channel_id=1, source_target_pairs={{0,4},{4,8},{8,12},{12,14},{14,10},{10,6},{6,2},{2,0},{1,5},{5,9},... | collective-permute-start | bytes 3145736 | tf_op jit(solution)/shard_map/ppermute | solution.py:435
  3.7 26.4 %collective-permute-start.1 = (bf16[512,1024]{1,0:T(8,128)(2,1)}, bf16[512,1024]{1,0:T(8,128)(2,1)}, u32[]{:S(2)}, u32[]{:S(2)}) collective-permute-start(bf16[512,1024]{1,0:T(8,128)(2,1)} %refs_0_.3), channel_id=1, source_target_pairs={{4,0},{8,4},{12,8},{14,12},{10,14},{6,10},{2,6},{0,2},{5,1},{9,5},... | collective-permute-start | bytes 3145736 | tf_op jit(solution)/shard_map/ppermute | solution.py:435
  3.7 1.2 copy-start.9
  6.8 43.3 %all-to-all-start = ((bf16[8,16,2560]{2,1,0:T(8,128)(2,1)}), bf16[8,16,2560]{2,1,0:T(8,128)(2,1)}, u32[]{:S(2)}, u32[]{:S(2)}) async-start(bf16[8,16,2560]{2,1,0:T(8,128)(2,1)} %shard_map.112.refs_3_), calls=%async_computation | async-start | bytes 1310720 | tf_op jit(solution)/shard_map/all_to_all | solution.py:438
  14.4 1.2 copy-start.2
  15.6 1.2 copy-start.6
  30.1 32.4 %collective-permute-start.2 = (bf16[512,1024]{1,0:T(8,128)(2,1)}, bf16[512,1024]{1,0:T(8,128)(2,1)S(1)}, u32[]{:S(2)}, u32[]{:S(2)}) collective-permute-start(bf16[512,1024]{1,0:T(8,128)(2,1)} %get-tuple-element.42.refs_0_.refs_1_), channel_id=1, source_target_pairs={{0,4},{4,8},{8,12},{12,14},{14,10},{10,6},{6,2},{2,0},{1,5},{5,9},... | collective-permute-start | bytes 3145736 | tf_op jit(solution)/shard_map/ppermute | solution.py:435
  31.8 30.7 %collective-permute-start.3 = (bf16[512,1024]{1,0:T(8,128)(2,1)}, bf16[512,1024]{1,0:T(8,128)(2,1)S(1)}, u32[]{:S(2)}, u32[]{:S(2)}) collective-permute-start(bf16[512,1024]{1,0:T(8,128)(2,1)} %get-tuple-element.43.refs_1_.refs_2_), channel_id=1, source_target_pairs={{4,0},{8,4},{12,8},{14,12},{10,14},{6,10},{2,6},{0,2},{5,1},{9,5},... | collective-permute-start | bytes 3145736 | tf_op jit(solution)/shard_map/ppermute | solution.py:435
  32.1 20.3 %copy-start.11 = (s32[512,1]{0,1:T(1,128)S(1)}, s32[512,1]{0,1:T(1,128)}, u32[]{:S(2)}) copy-start(s32[512,1]{0,1:T(1,128)} %param.15) | copy-start | bytes 6148
  32.1 20.3 %copy-start.12 = (s32[8]{0:T(128)S(1)}, s32[8]{0:T(128)}, u32[]{:S(2)}) copy-start(s32[8]{0:T(128)} %owner_ref.3) | copy-start | bytes 100
  46.7 3.3 %copy-start = (f32[4096,512]{1,0:T(8,128)}, f32[4096,512]{1,0:T(8,128)S(1)}, u32[]{:S(2)}) copy-start(f32[4096,512]{1,0:T(8,128)S(1)} %get-tuple-element.49.refs_6_) | copy-start | bytes 25165828
  50.0 24.1 %copy-start.3 = (bf16[64,8192]{1,0:T(8,128)(2,1)S(1)}, bf16[64,8192]{1,0:T(8,128)(2,1)}, u32[]{:S(2)}) copy-start(bf16[64,8192]{1,0:T(8,128)(2,1)} %refs_2_.9) | copy-start | bytes 3145732
  50.0 24.1 %copy-start.1 = (f32[4096,512]{1,0:T(8,128)S(1)}, f32[4096,512]{1,0:T(8,128)}, u32[]{:S(2)}) copy-start(f32[4096,512]{1,0:T(8,128)} %copy-done) | copy-start | bytes 25165828
  50.0 2.4 %collective-permute-start.4 = (bf16[8,16,2560]{2,1,0:T(8,128)(2,1)}, bf16[8,16,2560]{2,1,0:T(8,128)(2,1)S(1)}, u32[]{:S(2)}, u32[]{:S(2)}) collective-permute-start(bf16[8,16,2560]{2,1,0:T(8,128)(2,1)} %shard_map.116.own_ref), channel_id=1, source_target_pairs={{0,1},{1,0},{2,3},{3,2},{4,5},{5,4},{6,7},{7,6},{8,9},{9,8},{10,11... | collective-permute-start | bytes 1966088 | tf_op jit(solution)/shard_map/ppermute | solution.py:455
  52.4 2.5 %copy-start.4 = (bf16[512,4096]{1,0:T(8,128)(2,1)S(1)}, bf16[512,4096]{1,0:T(8,128)(2,1)}, u32[]{:S(2)}) copy-start(bf16[512,4096]{1,0:T(8,128)(2,1)} %act_ref.3) | copy-start | bytes 12582916
  59.2 8.4 %collective-permute-start.7 = (f32[5,16,512]{2,1,0:T(8,128)S(1)}, f32[5,16,512]{2,1,0:T(8,128)S(1)}, u32[]{:S(2)}, u32[]{:S(2)}) collective-permute-start(f32[5,16,512]{2,1,0:T(8,128)S(1)} %get-tuple-element.51), channel_id=1, source_target_pairs={{0,2},{2,0},{4,6},{6,4},{8,10},{10,8},{12,14},{14,12},{1,3},{3,1},... | collective-permute-start | bytes 491528 | tf_op jit(solution)/shard_map/ppermute | solution.py:442
  62.5 33.3 %collective-permute-start.5 = (bf16[512,1024]{1,0:T(8,128)(2,1)S(1)}, bf16[512,1024]{1,0:T(8,128)(2,1)S(1)}, u32[]{:S(2)}, u32[]{:S(2)}) collective-permute-start(bf16[512,1024]{1,0:T(8,128)(2,1)S(1)} %get-tuple-element.47.after.refs_0_.refs_3_), channel_id=1, source_target_pairs={{0,4},{4,8},{8,12},{12,14},{14,10},{10,6},{6,2},{2,0},{1,5},{5,9},... | collective-permute-start | bytes 3145736 | tf_op jit(solution)/shard_map/ppermute | solution.py:435
  67.6 23.1 %collective-permute-start.10 = (f32[32,512]{1,0:T(8,128)S(1)}, f32[32,512]{1,0:T(8,128)S(1)}, u32[]{:S(2)}, u32[]{:S(2)}) collective-permute-start(f32[32,512]{1,0:T(8,128)S(1)} %get-tuple-element.57), channel_id=1, source_target_pairs={{0,4},{2,6},{4,0},{6,2},{8,12},{10,14},{12,8},{14,10},{1,5},{3,7},... | collective-permute-start | bytes 196616 | tf_op jit(solution)/shard_map/ppermute | solution.py:442
  69.5 21.9 %collective-permute-start.11 = (f32[32,512]{1,0:T(8,128)S(1)}, f32[32,512]{1,0:T(8,128)S(1)}, u32[]{:S(2)}, u32[]{:S(2)}) collective-permute-start(f32[32,512]{1,0:T(8,128)S(1)} %get-tuple-element.58), channel_id=1, source_target_pairs={{0,8},{2,10},{4,12},{6,14},{8,0},{10,2},{12,4},{14,6},{1,9},{3,11}... | collective-permute-start | bytes 196616 | tf_op jit(solution)/shard_map/ppermute | solution.py:442
  71.3 20.8 %collective-permute-start.12 = (f32[32,512]{1,0:T(8,128)S(1)}, f32[32,512]{1,0:T(8,128)S(1)}, u32[]{:S(2)}, u32[]{:S(2)}) collective-permute-start(f32[32,512]{1,0:T(8,128)S(1)} %get-tuple-element.59), channel_id=1, source_target_pairs={{0,12},{2,14},{4,8},{6,10},{8,4},{10,6},{12,0},{14,2},{1,13},{3,15... | collective-permute-start | bytes 196616 | tf_op jit(solution)/shard_map/ppermute | solution.py:442
  72.4 25.9 %collective-permute-start.6 = (bf16[512,1024]{1,0:T(8,128)(2,1)S(1)}, bf16[512,1024]{1,0:T(8,128)(2,1)S(1)}, u32[]{:S(2)}, u32[]{:S(2)}) collective-permute-start(bf16[512,1024]{1,0:T(8,128)(2,1)S(1)} %get-tuple-element.48.refs_1_.refs_4_), channel_id=1, source_target_pairs={{4,0},{8,4},{12,8},{14,12},{10,14},{6,10},{2,6},{0,2},{5,1},{9,5},... | collective-permute-start | bytes 3145736 | tf_op jit(solution)/shard_map/ppermute | solution.py:435
  74.1 18.0 %copy-start.5 = (bf16[512,4096]{1,0:T(8,128)(2,1)S(1)}, bf16[512,4096]{1,0:T(8,128)(2,1)}, u32[]{:S(2)}) copy-start(bf16[512,4096]{1,0:T(8,128)(2,1)} %act_ref.3) | copy-start | bytes 12582916
  74.1 19.4 %copy-start.8 = (bf16[512,1024]{1,0:T(8,128)(2,1)S(1)}, bf16[512,1024]{1,0:T(8,128)(2,1)}, u32[]{:S(2)}) copy-start(bf16[512,1024]{1,0:T(8,128)(2,1)} %refs_0_.3) | copy-start | bytes 3145732
  93.4 7.7 %collective-permute-start.13 = (f32[8,16,2048]{2,1,0:T(8,128)S(1)}, f32[8,16,2048]{2,1,0:T(8,128)S(1)}, u32[]{:S(2)}, u32[]{:S(2)}) collective-permute-start(f32[8,16,2048]{2,1,0:T(8,128)S(1)} %get-tuple-element.63), channel_id=1, source_target_pairs={{0,1},{1,0},{2,3},{3,2},{4,5},{5,4},{6,7},{7,6},{8,9},{9,8},{10,11... | collective-permute-start | bytes 3145736 | tf_op jit(solution)/shard_map/ppermute | solution.py:467
  98.3 26.7 %collective-permute-start.8 = (bf16[256,1024]{1,0:T(8,128)(2,1)S(1)}, bf16[256,1024]{1,0:T(8,128)(2,1)S(1)}, u32[]{:S(2)}, u32[]{:S(2)}) collective-permute-start(bf16[256,1024]{1,0:T(8,128)(2,1)S(1)} %get-tuple-element.54), channel_id=1, source_target_pairs={{0,4},{4,8},{8,12},{12,14},{14,10},{10,6},{6,2},{2,0},{1,5},{5,9},... | collective-permute-start | bytes 1572872 | tf_op jit(solution)/shard_map/ppermute | solution.py:435
  101.1 26.4 %collective-permute-start.9 = (bf16[256,1024]{1,0:T(8,128)(2,1)S(1)}, bf16[256,1024]{1,0:T(8,128)(2,1)S(1)}, u32[]{:S(2)}, u32[]{:S(2)}) collective-permute-start(bf16[256,1024]{1,0:T(8,128)(2,1)S(1)} %get-tuple-element.55), channel_id=1, source_target_pairs={{4,0},{8,4},{12,8},{14,12},{10,14},{6,10},{2,6},{0,2},{5,1},{9,5},... | collective-permute-start | bytes 1572872 | tf_op jit(solution)/shard_map/ppermute | solution.py:435
  101.2 16.4 %collective-permute-start.14 = (bf16[4,16,2048]{2,1,0:T(8,128)(2,1)S(1)}, bf16[4,16,2048]{2,1,0:T(8,128)(2,1)S(1)}, u32[]{:S(2)}, u32[]{:S(2)}) collective-permute-start(bf16[4,16,2048]{2,1,0:T(8,128)(2,1)S(1)} %get-tuple-element.72), channel_id=1, source_target_pairs={{0,2},{2,0},{4,6},{6,4},{8,10},{10,8},{12,14},{14,12},{1,3},{3,1},... | collective-permute-start | bytes 786440 | tf_op jit(solution)/shard_map/ppermute | solution.py:442
  117.6 20.9 %collective-permute-start.15 = (bf16[2,16,2048]{2,1,0:T(8,128)(2,1)S(1)}, bf16[2,16,2048]{2,1,0:T(8,128)(2,1)S(1)}, u32[]{:S(2)}, u32[]{:S(2)}) collective-permute-start(bf16[2,16,2048]{2,1,0:T(8,128)(2,1)S(1)} %get-tuple-element.73), channel_id=1, source_target_pairs={{0,0},{1,4},{2,2},{3,6},{4,8},{5,12},{6,10},{7,14},{8,1},{9,5},{10... | collective-permute-start | bytes 393224 | tf_op jit(solution)/shard_map/ppermute | solution.py:482
  118.3 20.3 %collective-permute-start.16 = (bf16[2,16,2048]{2,1,0:T(8,128)(2,1)S(1)}, bf16[2,16,2048]{2,1,0:T(8,128)(2,1)S(1)}, u32[]{:S(2)}, u32[]{:S(2)}) collective-permute-start(bf16[2,16,2048]{2,1,0:T(8,128)(2,1)S(1)} %get-tuple-element.74), channel_id=1, source_target_pairs={{0,4},{1,0},{2,6},{3,2},{4,12},{5,8},{6,14},{7,10},{8,5},{9,1},{10... | collective-permute-start | bytes 393224 | tf_op jit(solution)/shard_map/ppermute | solution.py:482
  123.9 14.7 %collective-permute-start.17 = (bf16[2,16,2048]{2,1,0:T(8,128)(2,1)S(1)}, bf16[2,16,2048]{2,1,0:T(8,128)(2,1)S(1)}, u32[]{:S(2)}, u32[]{:S(2)}) collective-permute-start(bf16[2,16,2048]{2,1,0:T(8,128)(2,1)S(1)} %get-tuple-element.75), channel_id=1, source_target_pairs={{0,8},{1,12},{2,10},{3,14},{4,0},{5,4},{6,2},{7,6},{8,9},{9,13},{1... | collective-permute-start | bytes 393224 | tf_op jit(solution)/shard_map/ppermute | solution.py:482
  125.0 13.5 %collective-permute-start.18 = (bf16[2,16,2048]{2,1,0:T(8,128)(2,1)S(1)}, bf16[2,16,2048]{2,1,0:T(8,128)(2,1)S(1)}, u32[]{:S(2)}, u32[]{:S(2)}) collective-permute-start(bf16[2,16,2048]{2,1,0:T(8,128)(2,1)S(1)} %get-tuple-element.76), channel_id=1, source_target_pairs={{0,12},{1,8},{2,14},{3,10},{4,4},{5,0},{6,6},{7,2},{8,13},{9,9},{1... | collective-permute-start | bytes 393224 | tf_op jit(solution)/shard_map/ppermute | solution.py:482
  128.4 11.2 %collective-permute-start.19 = (f32[16,4096]{1,0:T(8,128)S(1)}, f32[16,4096]{1,0:T(8,128)S(1)}, u32[]{:S(2)}, u32[]{:S(2)}) collective-permute-start(f32[16,4096]{1,0:T(8,128)S(1)} %get-tuple-element.78), channel_id=1, source_target_pairs={{0,1},{1,0},{2,3},{3,2},{4,5},{5,4},{6,7},{7,6},{8,9},{9,8},{10,11... | collective-permute-start | bytes 786440 | tf_op jit(solution)/shard_map/ppermute | solution.py:485
  (2 other events, 2.2 us)
